TPU v7x, 128 devices: a whole 4x4x4 slice. The times are simulated.
128 devices in a mesh: grp: 2 (over y_lo), seq: 16 (over z, y_hi, core), tile: 4 (over x).
Axes of the slice: x: 4, y: 4 (y_hi: 2, y_lo: 2; y = y_hi * 2 + y_lo), z: 4, core: 2. Of those that a mesh axis runs over, the one named last changes fastest.
Arguments:
- tokens: bfloat16 [2, 64, 128, 2432], P('grp', 'seq'), may hold values from -6 to 6
- shift: float32 [2, 2432], P('grp'), may hold values from -3 to 3
- scale: float32 [2, 2432], P('grp'), may hold values from -3 to 3
- gate: float32 [2, 2432], P('grp'), may hold values from -4 to 4
- fc1: bfloat16 [2432, 5120], P(('grp', 'seq'), 'tile'), may hold values from -0.125 to 0.125
- fc2: bfloat16 [5120, 2432], P('tile', ('grp', 'seq')), may hold values from -0.078125 to 0.078125
- proj: bfloat16 [2432, 64], replicated, may hold values from -0.125 to 0.125
- lift: bfloat16 [16, 256], replicated, may hold values from -1.5 to 1.5
- conv_a: bfloat16 [3, 3, 256, 256], replicated, may hold values from -0.125 to 0.125
- conv_b: bfloat16 [3, 3, 256, 256], replicated, may hold values from -0.125 to 0.125
- target: bfloat16 [2, 256, 512, 256], P('grp', 'seq', 'tile'), may hold values from -6 to 6
Outputs:
- grad_fc1: float32 [2432, 5120], P(('grp', 'seq'), 'tile')
- grad_fc2: float32 [5120, 2432], P('tile', ('grp', 'seq'))
- latent_grad: float32 [2, 64, 128, 64], P('grp', 'seq', 'tile')
All inputs are finite; a program needn't handle non-finite values.
Results may differ from a plain program's by a relative error of at most 0.02.
Values may be sent and summed in bfloat16 or wider, within the bound.
A program may use at most 128 MiB of HBM per device.

v0:
```python
import jax
import jax.numpy as jnp
from jax import lax
from jax.sharding import PartitionSpec as P


def padded_2(x, sides, width):
    for axis, dim in sides:
        size, length = (lax.axis_size(axis), x.shape[dim])
        up = [(i, (i + 1) % size) for i in range(size - 1)]
        down = [(j, i) for i, j in up]
        last = lax.slice_in_dim(x, length - width, length, axis=dim)
        leading = lax.slice_in_dim(x, 0, width, axis=dim)
        before = lax.ppermute(last, axis, up)
        after = lax.ppermute(leading, axis, down)
        x = jnp.concatenate([before, x, after], axis=dim)
    return x


def gelu_tanh(value):
    return jax.nn.gelu(value, approximate=True)


def conv_tile(padded, kernel):
    height = padded.shape[0] - 2
    width = padded.shape[1] - 2
    total = jnp.zeros((height, width, kernel.shape[3]), jnp.float32)
    for row_off in range(3):
        for col_off in range(3):
            window = padded[row_off : row_off + height, col_off : col_off + width]
            total = total + jnp.dot(
                window, kernel[row_off, col_off], preferred_element_type=jnp.float32
            )
    return total


def flipped(kernel):
    return jnp.swapaxes(kernel[::-1, ::-1], 2, 3)


def bordered(value):
    return padded_2(value, (("seq", 0), ("tile", 1)), 1)


def doubled(value):
    return jnp.repeat(jnp.repeat(value, 2, axis=0), 2, axis=1)


def unpatch(patch):
    rows, cols = (patch.shape[0], patch.shape[1])
    return (
        patch.reshape(rows, cols, 2, 2, -1).transpose(0, 2, 1, 3, 4).reshape(2 * rows, 2 * cols, -1)
    )


def repatch(latent):
    rows, cols = (latent.shape[0] // 2, latent.shape[1] // 2)
    return latent.reshape(rows, 2, cols, 2, -1).transpose(0, 2, 1, 3, 4).reshape(rows, cols, -1)


def shards(tokens, shift, scale, gate, fc1, fc2, proj, lift, conv_a, conv_b, target):
    tok_here, tok_cols, width = (tokens.shape[1], tokens.shape[2], tokens.shape[3])
    rows_x = tokens[0].reshape(-1, width)
    proj_full = proj.astype(jnp.float32)
    lift_full = lift.astype(jnp.float32)
    xfull = rows_x.astype(jnp.float32)
    center = xfull - jnp.mean(xfull, axis=1, keepdims=True)
    spread = jnp.mean(center * center, axis=1, keepdims=True)
    normed = (center * lax.rsqrt(spread + 1e-06) * (1.0 + scale[0]) + shift[0]).astype(jnp.bfloat16)
    fc1_all, fc2_all = (
        lax.all_gather(fc1, ("grp", "seq"), axis=0, tiled=True),
        lax.all_gather(fc2, ("grp", "seq"), axis=1, tiled=True),
    )
    pre = jnp.dot(normed, fc1_all, preferred_element_type=jnp.float32)
    act = gelu_tanh(pre).astype(jnp.bfloat16)
    mlp = jnp.dot(act, fc2_all, preferred_element_type=jnp.float32)
    partial_value = jnp.dot(gate[0] * mlp, proj_full, precision=lax.Precision.HIGHEST).reshape(
        tok_here, tok_cols, -1
    )
    col_count = tok_cols // lax.axis_size("tile")
    col_start = lax.axis_index("tile") * col_count
    summed = lax.psum(partial_value.astype(jnp.bfloat16), "tile").astype(jnp.float32)
    mine = lax.dynamic_slice_in_dim(summed, col_start, col_count, 1)
    x_mine = lax.dynamic_slice_in_dim(tokens[0], col_start, col_count, 1)
    patch = jnp.dot(x_mine, proj, preferred_element_type=jnp.float32) + mine
    latent = unpatch(patch).astype(jnp.bfloat16)
    lifted = jnp.dot(latent, lift, preferred_element_type=jnp.float32).astype(jnp.bfloat16)
    padded = bordered(doubled(lifted))
    first = conv_tile(padded, conv_a)
    smooth = jax.nn.silu(first).astype(jnp.bfloat16)
    decoded = conv_tile(bordered(smooth), conv_b)
    grad_decoded = (decoded - target[0].astype(jnp.float32)).astype(jnp.bfloat16)
    grad_smooth = conv_tile(bordered(grad_decoded), flipped(conv_b))
    sigma = jax.nn.sigmoid(first)
    grad_first = (grad_smooth * sigma * (1.0 + first * (1.0 - sigma))).astype(jnp.bfloat16)
    grad_up = conv_tile(bordered(grad_first), flipped(conv_a))
    height, breadth = (grad_up.shape[0] // 2, grad_up.shape[1] // 2)
    grad_lifted = grad_up.reshape(height, 2, breadth, 2, -1).sum(axis=(1, 3))
    grad_latent = jnp.dot(grad_lifted, lift_full.T, precision=lax.Precision.HIGHEST)
    latent_mine = repatch(grad_latent)
    latent_rows = lax.all_gather(
        latent_mine.astype(jnp.bfloat16), "tile", axis=1, tiled=True
    ).astype(latent_mine.dtype)
    grad_mlp = (
        jnp.dot(
            latent_rows.reshape(-1, latent_rows.shape[-1]),
            proj_full.T,
            precision=lax.Precision.HIGHEST,
        )
        * gate[0]
    ).astype(jnp.bfloat16)
    grad_act = lax.dot_general(
        grad_mlp,
        lax.all_gather(fc2, ("grp", "seq"), axis=1, tiled=True),
        (((1,), (1,)), ((), ())),
        preferred_element_type=jnp.float32,
    )
    grad_pre = jax.vjp(gelu_tanh, pre)[1](grad_act)[0].astype(jnp.bfloat16)
    term_one = lax.dot_general(
        normed, grad_pre, (((0,), (0,)), ((), ())), preferred_element_type=jnp.float32
    )
    term_two = lax.dot_general(
        grad_mlp, act, (((0,), (0,)), ((), ())), preferred_element_type=jnp.float32
    )
    both = lax.psum_scatter(
        jnp.concatenate([term_one, term_two], axis=1).astype(jnp.bfloat16),
        ("grp", "seq"),
        scatter_dimension=0,
        tiled=True,
    ).astype(jnp.float32)
    hidden_here = fc1.shape[1]
    grad_one = both[:, :hidden_here]
    grad_two = both[:, hidden_here:].T
    return (grad_one, grad_two, latent_mine[None])


def solution(mesh):
    in_specs = (
        P("grp", "seq", None, None),
        P("grp", None),
        P("grp", None),
        P("grp", None),
        P(("grp", "seq"), "tile"),
        P("tile", ("grp", "seq")),
        P(),
        P(),
        P(),
        P(),
        P("grp", "seq", "tile", None),
    )
    out_specs = (
        P(("grp", "seq"), "tile"),
        P("tile", ("grp", "seq")),
        P("grp", "seq", "tile", None),
    )
    return jax.shard_map(shards, mesh=mesh, in_specs=in_specs, out_specs=out_specs, check_vma=False)
```

profile of v0, /device:TPU:1, one launch (start us, length us, event | category | flops | bytes accessed | tf_op | source)
XLA Modules:
  0.0 487.0 jit_solution(6305167442751822525)
XLA Ops:
  8.7 0.7 reduce.3
  9.4 0.7 reduce.4
  10.2 2.4 copy.36
  12.6 2.5 copy.37
  15.1 2.4 reverse_bitcast_fusion.1
  18.0 0.8 multiply_reduce_fusion
  18.8 2.4 fusion.3
  21.2 55.8 %all-gather.5.cloned.1.call-done = bf16[32,76,1280]{2,1,0:T(8,128)(2,1)} async-done(((bf16[1,76,1280]{2,1,0:T(8,128)(2,1)}), bf16[32,76,1280]{2,1,0:T(8,128)(2,1)}) %all-gather.5.cloned.1.call-update) | async-done | bytes 6225936 | tf_op jit(solution)/shard_map/all_gather | solution.py:71
  77.0 8.2 %reshape.84 = bf16[2432,1280]{1,0:T(8,128)(2,1)} reshape(bf16[32,76,1280]{2,1,0:T(8,128)(2,1)} %all-gather.5.cloned.1.call-done) | data formatting | bytes 12451840
  85.2 8.8 %fusion.186 = f32[512,1280]{1,0:T(8,128)} fusion(bf16[512,2432]{1,0:T(8,128)(2,1)} %fusion.3, bf16[2432,1280]{1,0:T(8,128)(2,1)} %reshape.84), kind=kOutput, calls=%fused_computation.251 | convolution fusion | flops 3187671040 | bytes 11337728 | tf_op jit(solution)/shard_map/dot_general | solution.py:74
  94.0 47.7 %all-gather.7.cloned.1.call-done = bf16[32,76,1280]{2,1,0:T(8,128)(2,1)} async-done(((bf16[1,76,1280]{2,1,0:T(8,128)(2,1)}), bf16[32,76,1280]{2,1,0:T(8,128)(2,1)}) %all-gather.7.cloned.1.call-update) | async-done | bytes 6225936 | tf_op jit(solution)/shard_map/all_gather | solution.py:72
  141.7 8.3 %reshape.86 = bf16[2432,1280]{1,0:T(8,128)(2,1)} reshape(bf16[32,76,1280]{2,1,0:T(8,128)(2,1)} %all-gather.7.cloned.1.call-done) | data formatting | bytes 12451840
  150.0 6.9 %convolution_multiply_fusion.1 = f32[512,2432]{1,0:T(8,128)S(1)} fusion(bf16[2432,1280]{1,0:T(8,128)(2,1)} %reshape.86, f32[2432]{0:T(1024)S(1)} %reduce.4, f32[512,1280]{1,0:T(8,128)} %fusion.186), kind=kOutput, calls=%fused_computation.4 | convolution fusion | flops 3194814464 | bytes 13837824 | tf_op jit(solution)/shard_map/dot_general | solution.py:76
  156.9 2.7 convolution_convert_fusion.3
  159.6 0.8 copy.32
  160.4 2.4 reverse_bitcast_fusion
  162.8 35.7 %all-reduce.4.cloned.1.call-done = bf16[4,128,64]{2,1,0:T(8,128)(2,1)} async-done(((bf16[4,128,64]{2,1,0:T(8,128)(2,1)}), bf16[4,128,64]{2,1,0:T(8,128)(2,1)}) %all-reduce.4.cloned.1.call-update) | async-done | bytes 65552 | tf_op jit(solution)/shard_map/psum | solution.py:82
  198.5 1.1 fusion.20
  200.1 1.8 broadcast_in_dim.20
  201.9 1.5 reshape.78
  203.5 7.7 %collective-permute-start = (bf16[1,128,256]{2,1,0:T(8,128)(2,1)S(1)}, bf16[1,128,256]{2,1,0:T(8,128)(2,1)S(1)}, u32[]{:S(2)}, u32[]{:S(2)}) collective-permute-start(bf16[1,128,256]{2,1,0:T(8,128)(2,1)S(1)} %broadcast_in_dim.19), channel_id=1, source_target_pairs={{0,4},{4,8},{8,12},{12,16},{16,20},{20,24},{24,28},{28,32},{32,36}... | collective-permute-start | bytes 196616 | tf_op jit(solution)/shard_map/ppermute | solution.py:14
  211.3 1.9 collective-permute-start.1
  213.7 4.6 collective-permute-done.1
  218.4 2.0 collective-permute-start.2
  220.4 1.3 collective-permute-start.3
  223.5 1.4 collective-permute-done.3
  226.3 1.3 multiply_convert_fusion.2
  227.6 3.3 collective-permute-start.4
  230.9 1.9 collective-permute-start.5
  233.3 4.7 collective-permute-done.5
  238.0 3.4 collective-permute-start.6
  241.4 1.3 collective-permute-start.7
  243.6 2.3 collective-permute-done.7
  245.9 0.8 pad_maximum_fusion.1
  249.0 0.8 copy-done.7
  249.8 1.5 fusion.12
  251.3 3.3 collective-permute-start.8
  254.6 1.9 collective-permute-start.9
  257.0 4.7 collective-permute-done.9
  261.7 2.5 collective-permute-start.10
  264.2 1.5 collective-permute-start.11
  266.6 2.1 collective-permute-done.11
  268.7 0.8 pad_maximum_fusion.2
  271.8 1.7 multiply_convert_fusion.1
  273.6 3.3 collective-permute-start.12
  276.9 1.9 collective-permute-start.13
  279.2 4.7 collective-permute-done.13
  284.0 1.7 collective-permute-start.14
  285.7 1.3 collective-permute-start.15
  287.9 2.3 collective-permute-done.15
  290.2 0.9 pad_maximum_fusion.3
  293.3 1.3 add_add_fusion
  294.6 2.2 reshape.79
  296.9 3.1 reduce_sum.29
  301.1 9.3 %all_gather.12 = bf16[4,128,64]{2,0,1:T(4,128)(2,1)S(1)} all-gather(bf16[4,32,64]{2,0,1:T(4,128)(2,1)S(1)} %copy.39), channel_id=1, replica_groups=mesh['grp'=2,'seq'=16,'tile'=4] {'tile'}, dimensions={1}, use_global_device_ids=true | all-gather | bytes 81920 | tf_op jit(solution)/shard_map/all_gather | solution.py:101
  310.5 0.8 fusion.4
  311.4 6.5 %fusion.187 = f32[512,1280]{1,0:T(8,128)S(1)} fusion(bf16[512,2432]{1,0:T(8,128)(2,1)S(1)} %fusion.4, bf16[2432,1280]{1,0:T(8,128)(2,1)} %reshape.86), kind=kOutput, calls=%fused_computation.252 | convolution fusion | flops 3187671040 | bytes 11337728 | tf_op jit(solution)/shard_map/dot_general | solution.py:112
  317.9 4.0 convolution_convert_fusion
  321.9 4.9 %convolution_convert_fusion.1 = bf16[2432,1280]{0,1:T(8,128)(2,1)S(1)} fusion(bf16[512,2432]{1,0:T(8,128)(2,1)S(1)} %copy-done.6, f32[512,1280]{1,0:T(8,128)S(1)} %copy-done.11, f32[512,1280]{1,0:T(8,128)S(1)} %fusion.187), kind=kOutput, calls=%fused_computation.2 | convolution fusion | flops 3203891200 | bytes 13959168 | tf_op jit(solution)/shard_map/dot_general | solution.py:119
  326.8 13.8 %pad_maximum_fusion = bf16[2432,2560]{0,1:T(8,128)(2,1)} fusion(bf16[2432,1280]{0,1:T(8,128)(2,1)S(1)} %convolution_convert_fusion, bf16[2432,1280]{0,1:T(8,128)(2,1)S(1)} %convolution_convert_fusion.1), kind=kLoop, calls=%fused_computation | loop fusion | flops 24903680 | bytes 24903680 | tf_op jit(solution)/shard_map/concatenate | solution.py:126
  343.2 133.4 %all-reduce.6.cloned.1.call-done = bf16[2432,2560]{0,1:T(8,128)(2,1)} async-done(((bf16[2432,2560]{0,1:T(8,128)(2,1)}), bf16[2432,2560]{0,1:T(8,128)(2,1)}) %all-reduce.6.cloned.1.call-update) | async-done | bytes 12451856
  476.6 1.6 dynamic-slice_convert_fusion
  478.3 1.0 copy.41
  479.3 1.0 copy.42
  (101 shorter events, 20.2 us)
Async XLA Ops:
  7.2 149.7 %copy-start = (bf16[2432,64]{0,1:T(8,128)(2,1)S(1)}, bf16[2432,64]{0,1:T(8,128)(2,1)}, u32[]{:S(2)}) copy-start(bf16[2432,64]{0,1:T(8,128)(2,1)} %param.17) | copy-start | bytes 933892
  7.2 69.8 %all-gather.5.cloned.1.call-start = ((), (), s32[]{:S(2)}) async-start(), calls=%async_computation.1 | async-start | bytes 6758400 | tf_op jit(solution)/shard_map/all_gather | solution.py:71
  7.9 133.8 %all-gather.7.cloned.1.call-start = ((), (), s32[]{:S(2)}) async-start(), calls=%async_computation.2 | async-start | bytes 6758400 | tf_op jit(solution)/shard_map/all_gather | solution.py:72
  8.7 189.9 %all-reduce.4.cloned.1.call-start = ((), (), s32[]{:S(2)}) async-start(), calls=%async_computation | async-start | bytes 262144 | tf_op jit(solution)/shard_map/psum | solution.py:82
  10.2 4.9 %copy-start.9 = (f32[1,2432]{1,0:T(1,128)S(1)}, f32[1,2432]{1,0:T(1,128)}, u32[]{:S(2)}) copy-start(f32[1,2432]{1,0:T(1,128)} %param.13) | copy-start | bytes 29188
  12.6 5.0 %copy-start.1 = (bf16[1,4,128,2432]{3,2,1,0:T(8,128)(2,1)S(1)}, bf16[1,4,128,2432]{3,2,1,0:T(8,128)(2,1)}, u32[]{:S(2)}) copy-start(bf16[1,4,128,2432]{3,2,1,0:T(8,128)(2,1)} %param.11) | copy-start | bytes 7471108
  159.6 40.3 %copy-start.8 = (bf16[16,256]{1,0:T(8,128)(2,1)S(1)}, bf16[16,256]{1,0:T(8,128)(2,1)}, u32[]{:S(2)}) copy-start(bf16[16,256]{1,0:T(8,128)(2,1)} %param.18) | copy-start | bytes 24580
  160.4 316.3 %all-reduce.6.cloned.1.call-start = ((), (), s32[]{:S(2)}) async-start(), calls=%async_computation.3 | async-start | bytes 24903680
  200.1 13.1 %copy-start.2 = (bf16[3,3,256,256]{3,2,1,0:T(8,128)(2,1)S(1)}, bf16[3,3,256,256]{3,2,1,0:T(8,128)(2,1)}, u32[]{:S(2)}) copy-start(bf16[3,3,256,256]{3,2,1,0:T(8,128)(2,1)} %param.19) | copy-start | bytes 3538948
  203.5 10.2 %collective-permute-start = (bf16[1,128,256]{2,1,0:T(8,128)(2,1)S(1)}, bf16[1,128,256]{2,1,0:T(8,128)(2,1)S(1)}, u32[]{:S(2)}, u32[]{:S(2)}) collective-permute-start(bf16[1,128,256]{2,1,0:T(8,128)(2,1)S(1)} %broadcast_in_dim.19), channel_id=1, source_target_pairs={{0,4},{4,8},{8,12},{12,16},{16,20},{20,24},{24,28},{28,32},{32,36}... | collective-permute-start | bytes 196616 | tf_op jit(solution)/shard_map/ppermute | solution.py:14
  211.3 7.1 %collective-permute-start.1 = (bf16[1,128,256]{2,1,0:T(8,128)(2,1)S(1)}, bf16[1,128,256]{2,1,0:T(8,128)(2,1)S(1)}, u32[]{:S(2)}, u32[]{:S(2)}) collective-permute-start(bf16[1,128,256]{2,1,0:T(8,128)(2,1)S(1)} %broadcast_in_dim.22), channel_id=1, source_target_pairs={{4,0},{8,4},{12,8},{16,12},{20,16},{24,20},{28,24},{32,28},{36,32}... | collective-permute-start | bytes 196616 | tf_op jit(solution)/shard_map/ppermute | solution.py:15
  218.4 4.2 collective-permute-start.2
  220.4 4.5 collective-permute-start.3
  226.3 6.6 %copy-start.3 = (bf16[3,3,256,256]{3,2,1,0:T(8,128)(2,1)S(1)}, bf16[3,3,256,256]{3,2,1,0:T(8,128)(2,1)}, u32[]{:S(2)}) copy-start(bf16[3,3,256,256]{3,2,1,0:T(8,128)(2,1)} %param.20) | copy-start | bytes 3538948
  227.6 5.7 %collective-permute-start.4 = (bf16[1,128,256]{2,1,0:T(8,128)(2,1)S(1)}, bf16[1,128,256]{2,1,0:T(8,128)(2,1)S(1)}, u32[]{:S(2)}, u32[]{:S(2)}) collective-permute-start(bf16[1,128,256]{2,1,0:T(8,128)(2,1)S(1)} %get-tuple-element.32), channel_id=1, source_target_pairs={{0,4},{4,8},{8,12},{12,16},{16,20},{20,24},{24,28},{28,32},{32,36}... | collective-permute-start | bytes 196616 | tf_op jit(solution)/shard_map/ppermute | solution.py:14
  230.9 7.1 %collective-permute-start.5 = (bf16[1,128,256]{2,1,0:T(8,128)(2,1)S(1)}, bf16[1,128,256]{2,1,0:T(8,128)(2,1)S(1)}, u32[]{:S(2)}, u32[]{:S(2)}) collective-permute-start(bf16[1,128,256]{2,1,0:T(8,128)(2,1)S(1)} %get-tuple-element.33), channel_id=1, source_target_pairs={{4,0},{8,4},{12,8},{16,12},{20,16},{24,20},{28,24},{32,28},{36,32}... | collective-permute-start | bytes 196616 | tf_op jit(solution)/shard_map/ppermute | solution.py:15
  238.0 5.6 %collective-permute-start.6 = (bf16[18,1,256]{2,1,0:T(2,128)(2,1)S(1)}, bf16[18,1,256]{2,1,0:T(2,128)(2,1)S(1)}, u32[]{:S(2)}, u32[]{:S(2)}) collective-permute-start(bf16[18,1,256]{2,1,0:T(2,128)(2,1)S(1)} %get-tuple-element.25), channel_id=1, source_target_pairs={{0,1},{1,2},{2,3},{4,5},{5,6},{6,7},{8,9},{9,10},{10,11},{12,13},{... | collective-permute-start | bytes 27656 | tf_op jit(solution)/shard_map/ppermute | solution.py:14
  241.4 4.5 collective-permute-start.7
  248.6 1.2 copy-start.7
  249.8 6.7 %copy-start.5 = (bf16[3,3,256,256]{3,2,1,0:T(8,128)(2,1)S(1)}, bf16[3,3,256,256]{3,2,1,0:T(8,128)(2,1)}, u32[]{:S(2)}) copy-start(bf16[3,3,256,256]{3,2,1,0:T(8,128)(2,1)} %reverse_bitcast_fusion.1) | copy-start | bytes 3538948
  251.3 5.7 %collective-permute-start.8 = (bf16[1,128,256]{2,1,0:T(8,128)(2,1)S(1)}, bf16[1,128,256]{2,1,0:T(8,128)(2,1)S(1)}, u32[]{:S(2)}, u32[]{:S(2)}) collective-permute-start(bf16[1,128,256]{2,1,0:T(8,128)(2,1)S(1)} %get-tuple-element.30), channel_id=1, source_target_pairs={{0,4},{4,8},{8,12},{12,16},{16,20},{20,24},{24,28},{28,32},{32,36}... | collective-permute-start | bytes 196616 | tf_op jit(solution)/shard_map/ppermute | solution.py:14
  254.6 7.1 %collective-permute-start.9 = (bf16[1,128,256]{2,1,0:T(8,128)(2,1)S(1)}, bf16[1,128,256]{2,1,0:T(8,128)(2,1)S(1)}, u32[]{:S(2)}, u32[]{:S(2)}) collective-permute-start(bf16[1,128,256]{2,1,0:T(8,128)(2,1)S(1)} %get-tuple-element.31), channel_id=1, source_target_pairs={{4,0},{8,4},{12,8},{16,12},{20,16},{24,20},{28,24},{32,28},{36,32}... | collective-permute-start | bytes 196616 | tf_op jit(solution)/shard_map/ppermute | solution.py:15
  261.7 4.9 %collective-permute-start.10 = (bf16[18,1,256]{2,1,0:T(2,128)(2,1)S(1)}, bf16[18,1,256]{2,1,0:T(2,128)(2,1)S(1)}, u32[]{:S(2)}, u32[]{:S(2)}) collective-permute-start(bf16[18,1,256]{2,1,0:T(2,128)(2,1)S(1)} %get-tuple-element.21), channel_id=1, source_target_pairs={{0,1},{1,2},{2,3},{4,5},{5,6},{6,7},{8,9},{9,10},{10,11},{12,13},{... | collective-permute-start | bytes 27656 | tf_op jit(solution)/shard_map/ppermute | solution.py:14
  264.2 4.5 collective-permute-start.11
  271.8 7.0 %copy-start.4 = (bf16[3,3,256,256]{3,2,1,0:T(8,128)(2,1)S(1)}, bf16[3,3,256,256]{3,2,1,0:T(8,128)(2,1)}, u32[]{:S(2)}) copy-start(bf16[3,3,256,256]{3,2,1,0:T(8,128)(2,1)} %reverse_bitcast_fusion) | copy-start | bytes 3538948
  273.6 5.7 %collective-permute-start.12 = (bf16[1,128,256]{2,1,0:T(8,128)(2,1)S(1)}, bf16[1,128,256]{2,1,0:T(8,128)(2,1)S(1)}, u32[]{:S(2)}, u32[]{:S(2)}) collective-permute-start(bf16[1,128,256]{2,1,0:T(8,128)(2,1)S(1)} %get-tuple-element.28), channel_id=1, source_target_pairs={{0,4},{4,8},{8,12},{12,16},{16,20},{20,24},{24,28},{28,32},{32,36}... | collective-permute-start | bytes 196616 | tf_op jit(solution)/shard_map/ppermute | solution.py:14
  276.9 7.1 %collective-permute-start.13 = (bf16[1,128,256]{2,1,0:T(8,128)(2,1)S(1)}, bf16[1,128,256]{2,1,0:T(8,128)(2,1)S(1)}, u32[]{:S(2)}, u32[]{:S(2)}) collective-permute-start(bf16[1,128,256]{2,1,0:T(8,128)(2,1)S(1)} %get-tuple-element.29), channel_id=1, source_target_pairs={{4,0},{8,4},{12,8},{16,12},{20,16},{24,20},{28,24},{32,28},{36,32}... | collective-permute-start | bytes 196616 | tf_op jit(solution)/shard_map/ppermute | solution.py:15
  284.0 3.9 collective-permute-start.14
  285.7 4.5 collective-permute-start.15
  311.4 6.5 %copy-start.11 = (f32[512,1280]{1,0:T(8,128)S(1)}, f32[512,1280]{1,0:T(8,128)}, u32[]{:S(2)}) copy-start(f32[512,1280]{1,0:T(8,128)} %fusion.186) | copy-start | bytes 7864324
  317.9 4.0 copy-start.6
  340.6 0.7 copy-start.10
Sparse Core Ops, SparseCore 0:
  9.7 67.2 all-gather.4
  78.7 62.9 all-gather.6
  160.5 37.9 all-reduce.3
  340.7 135.8 all-reduce.5
where the time goes:
time: 497 us; the launch traced here: 487 us
  waiting for transfers between devices  301 us (61%)
  matrix products  56.3 us (11%)
  starting transfers between devices  40.4 us (8%)
  local copies, waits for them, and re-layouts  38.3 us (8%)
  other arithmetic  26.3 us (5%)
  between operations  15.3 us (3%)
  blocking collectives  9.34 us (2%)
    unnamed x5, waiting for transfers between devices  135 us
    all_gather x1, waiting for transfers between devices, shards(): lax.all_gather(fc1, ('grp', 'seq'), axis=0, tiled=True)  55.8 us
    all_gather x1, waiting for transfers between devices, shards(): lax.all_gather(fc2, ('grp', 'seq'), axis=1, tiled=True)  47.7 us
    psum x1, waiting for transfers between devices, shards(): lax.psum(partial_value.astype(jnp.bfloat16), 'tile').astype(jnp.float32)  35.7 us
    ppermute x8, starting transfers between devices, padded_2(): before = lax.ppermute(last, axis, up)  27.2 us
    ppermute x8, waiting for transfers between devices, padded_2(): after = lax.ppermute(leading, axis, down)  27 us
    unnamed x34, local copies, waits for them, and re-layouts  26.2 us
    dot_general x36, matrix products, conv_tile(): jnp.dot(window, kernel[row_off, col_off], preferred_element_type=jnp.floa...  19.9 us
  transfers between devices with their start and end apart: 20, of which 12 were waited for; matrix products, arithmetic and copies ran while one was open for 8% of the time, Pallas kernels for 0%

commit v1 on v0

v1 whole, which is shorter than its diff:
```python
import jax
import jax.numpy as jnp
from jax import lax
from jax.experimental import pallas as pl
from jax.experimental.pallas import tpu as pltpu
from jax.sharding import PartitionSpec as P

F32 = jnp.float32
BF16 = jnp.bfloat16


def gelu_tanh(value):
    return jax.nn.gelu(value, approximate=True)


def split(value):
    high = value.astype(BF16)
    return high, (value - high.astype(F32)).astype(BF16)


MESH = pl.DeviceIdType.MESH
VMEM = pltpu.VMEM


def place():
    grp, seq, tile = lax.axis_index("grp"), lax.axis_index("seq"), lax.axis_index("tile")
    core = seq % 2
    y = (seq // 2) % 2 * 2 + grp
    z = seq // 4

    def device(y, z, core):
        return (y % 2, z * 4 + y // 2 * 2 + core, tile)

    return y, z, core, device


def oriented(y, z, core):
    a = y + core * (z - y)
    b = z + core * (y - z)

    def turn(a, b):
        return a + core * (b - a), b + core * (a - b)

    return a, b, turn


def block_of(y, z):
    return y % 2 * 8 + z * 2 + y // 2


def greet(peers):
    barrier = pltpu.get_barrier_semaphore()
    for peer in peers:
        pl.semaphore_signal(barrier, inc=1, device_id=peer, device_id_type=MESH)
    pl.semaphore_wait(barrier, len(peers))


def plane_peers(y, z, core, device):
    return (
        [device(y, z, 1 - core)]
        + [device((y + d) % 4, z, core) for d in range(1, 4)]
        + [device(y, (z + d) % 4, core) for d in range(1, 4)]
    )


def tile_peer(ds, dt):
    grp, seq, tile = lax.axis_index("grp"), lax.axis_index("seq"), lax.axis_index("tile")
    return (grp, (seq + ds) % 16, (tile + dt) % 4)


AROUND = [(0, 1), (0, 2), (0, 3)] + [(ds, dt) for ds in (-1, 1) for dt in range(4)]
NEXT = [(1, 0), (-1, 0), (0, 1), (0, -1), (1, 1), (1, -1), (-1, 1), (-1, -1)]
EDGE = 8
LEAD = 16


class Courier:
    def __init__(self, send, recv):
        self.send, self.recv, self.used, self.started = send, recv, 0, []

    def slot(self):
        self.used += 1
        return self.used - 1

    def copy(self, slot, src, dst, peer):
        return pltpu.make_async_remote_copy(
            src_ref=src,
            dst_ref=dst,
            send_sem=self.send.at[slot],
            recv_sem=self.recv.at[slot],
            device_id=peer,
            device_id_type=MESH,
        )

    def start(self, slot, src, dst, peer):
        copy = self.copy(slot, src, dst, peer)
        copy.start()
        self.started.append(copy)

    def arrived(self, slot, dst, peer):
        self.copy(slot, dst, dst, peer).wait_recv()

    def finish(self):
        for copy in self.started:
            copy.wait_send()


def forward_kernel(
    nrm, nrmt, fc1, fc2, gps, target, pre, act, part, fold, gboth, sibt, t_rows, t_cols, t_ends,
    gath, gin, wpart, wsib, wsum, wz_out, wz_in, wy_out, wy_in, wfull, send, recv,
):
    y, z, core, device = place()
    a, b, turn = oriented(y, z, core)
    grp = lax.axis_index("grp")
    other = 1 - core
    sibling = device(y, z, other)
    greet(plane_peers(y, z, core, device) + [tile_peer(ds, dt) for ds, dt in NEXT])
    mail = Courier(send, recv)
    rows, half = gath.shape[2] // 2, gath.shape[3]

    def peer(da, db):
        return device(*turn((a + da) % 4, (b + db) % 4), core)

    def block(da, db):
        return block_of(*turn((a + da) % 4, (b + db) % 4))

    own = block(0, 0)
    mine = pl.ds(pl.multiple_of(core * rows, 16), rows)
    theirs = pl.ds(pl.multiple_of(other * rows, 16), rows)
    for h in range(2):
        gath[h, own, mine, :] = fc1[:, h * half : (h + 1) * half]
    s_for, s_rest = mail.slot(), mail.slot()
    mail.start(s_for, gath.at[other, own, mine], gath.at[other, own, mine], sibling)
    mail.start(s_rest, gath.at[core, own, mine], gath.at[core, own, mine], sibling)
    s_nrm = mail.slot()
    mail.start(s_nrm, nrmt, sibt, sibling)
    partner = device(y // 2 * 2 + 1 - grp, z, core)
    s_gate = mail.slot()
    mail.start(s_gate, gps.at[1], gin, partner)

    top, bottom = pl.ds(0, rows), pl.ds(rows, rows)

    def held(da, db, where=None):
        ref = gath.at[core, block(da, db)]
        return ref if where is None else ref.at[where]

    def put(slot, da, db, to, where=None):
        mail.start(slot, held(da, db, where), held(da, db, where), peer(*to))

    def take(slot, da, db, frm, where=None):
        mail.arrived(slot, held(da, db, where), peer(*frm))

    def share(slot, da, db):
        mail.start(slot, held(da, db), held(da, db), sibling)

    def other_block(da, db):
        return gath.at[other, block(da, db)]

    def multiply(h, da, db, first=False):
        at = block(da, db)
        term = jnp.dot(nrm[at], gath[h, at], preferred_element_type=F32)
        pre[h] = term if first else pre[h] + term

    height, breadth = target.shape[0], target.shape[1]
    top_rows, end_rows = pl.ds(0, 2), pl.ds(height - 2, 2)
    lead, trail = pl.ds(0, LEAD), pl.ds(breadth - LEAD, LEAD)
    borders = {
        (1, 0): (target.at[end_rows], t_rows.at[0]),
        (-1, 0): (target.at[top_rows], t_rows.at[1]),
        (0, 1): (target.at[:, trail], t_cols.at[0]),
        (0, -1): (target.at[:, lead], t_cols.at[1]),
        (1, 1): (target.at[end_rows, trail], t_ends.at[0]),
        (1, -1): (target.at[end_rows, lead], t_ends.at[1]),
        (-1, 1): (target.at[top_rows, trail], t_ends.at[2]),
        (-1, -1): (target.at[top_rows, lead], t_ends.at[3]),
    }
    s_border = {to: mail.slot() for to in NEXT}
    for to in NEXT:
        mail.start(s_border[to], *borders[to], tile_peer(*to))

    A_UP, A_DOWN, A_UP2, A_DOWN2 = (mail.slot() for _ in range(4))
    sh = {}
    for da in range(4):
        for db in range(4):
            if (da, db) != (0, 0):
                sh[da, db] = mail.slot()
    bs = {(da, k): mail.slot() for da in range(4) for k in range(4)}

    mail.arrived(s_for, gath.at[core, own, theirs], sibling)
    put(A_UP, 0, 0, (1, 0))
    put(A_DOWN, 0, 0, (-1, 0))
    put(bs[0, 0], 0, 0, (0, 1))
    put(bs[0, 1], 0, 0, (0, -1))

    mail.arrived(s_gate, gin, partner)
    both = gps[0] + gin[...]
    gboth[...] = both
    high, low = split(both)
    wpart[...] = jnp.dot(fc2[...], high, preferred_element_type=F32) + jnp.dot(
        fc2[...], low, preferred_element_type=F32
    )
    wh = wpart.shape[0] // 2
    wq = wh // 4
    s_w = mail.slot()
    mail.start(s_w, wpart.at[pl.ds(pl.multiple_of(other * wh, 16), wh)], wsib, sibling)

    multiply(core, 0, 0, first=True)
    mail.arrived(s_rest, gath.at[other, own, theirs], sibling)
    multiply(other, 0, 0, first=True)

    take(A_UP, -1, 0, (-1, 0))
    put(A_UP2, -1, 0, (1, 0), top)
    take(A_DOWN, 1, 0, (1, 0))
    put(A_DOWN2, 1, 0, (-1, 0), bottom)
    for da in (3, 1):
        put(bs[da, 0], da, 0, (0, 1))
        put(bs[da, 1], da, 0, (0, -1))
        share(sh[da, 0], da, 0)

    mail.arrived(s_w, wsib, sibling)
    wsum[...] = wpart[pl.ds(pl.multiple_of(core * wh, 16), wh), :] + wsib[...]
    wz_out[...] = wsum[...].astype(BF16)
    s_wz = [mail.slot() for _ in range(3)]
    for d in range(1, 4):
        to = (z + d) % 4
        src = wz_out.at[pl.ds(pl.multiple_of(to * wq, 16), wq)]
        mail.start(s_wz[d - 1], src, wz_in.at[d - 1], device(y, to, core))

    multiply(core, -1, 0)
    multiply(core, 1, 0)

    def from_b(da):
        take(bs[da, 0], da, -1, (0, -1))
        put(bs[da, 2], da, -1, (0, 1), top)
        share(sh[da, 3], da, -1)
        take(bs[da, 1], da, 1, (0, 1))
        put(bs[da, 3], da, 1, (0, -1), bottom)
        share(sh[da, 1], da, 1)

    def from_b2(da):
        take(bs[da, 2], da, 2, (0, -1), top)
        take(bs[da, 3], da, 2, (0, 1), bottom)
        share(sh[da, 2], da, 2)

    def from_sibling(da, db):
        mail.arrived(sh[da, db], other_block(db, da), sibling)
        multiply(other, db, da)

    from_b(0)
    take(A_UP2, 2, 0, (-1, 0), top)
    take(A_DOWN2, 2, 0, (1, 0), bottom)
    put(bs[2, 0], 2, 0, (0, 1))
    put(bs[2, 1], 2, 0, (0, -1))
    share(sh[2, 0], 2, 0)

    for d in range(1, 4):
        mail.arrived(s_wz[d - 1], wz_in.at[d - 1], device(y, (z + 4 - d) % 4, core))
    here = pl.ds(pl.multiple_of(z * wq, 16), wq)
    total = wsum[here, :]
    for d in range(3):
        total = total + wz_in[d].astype(F32)
    wy_out[...] = total.astype(BF16)
    s_wy = [mail.slot() for _ in range(3)]
    for d in range(1, 4):
        mail.start(s_wy[d - 1], wy_out, wy_in.at[d - 1], device((y + d) % 4, z, core))

    multiply(core, 0, -1)
    multiply(core, 0, 1)
    multiply(core, 2, 0)
    from_b2(0)
    multiply(core, 0, 2)
    from_b(3)
    for d in range(1, 4):
        mail.arrived(s_wy[d - 1], wy_in.at[d - 1], device((y + 4 - d) % 4, z, core))
    for d in range(3):
        total = total + wy_in[d].astype(F32)
    where_w = pl.ds(pl.multiple_of(core * wh + z * wq, 16), wq)
    wfull[where_w, :] = total.astype(BF16)
    s_wa = [mail.slot() for _ in range(3)]
    for d in range(1, 4):
        mail.start(
            s_wa[d - 1], wfull.at[where_w], wfull.at[where_w], device(y, (z + d) % 4, core)
        )
    from_sibling(3, 0)
    from_sibling(1, 0)
    multiply(core, 3, -1)
    multiply(core, 3, 1)
    from_b2(3)
    from_b(1)
    from_sibling(0, 3)
    from_sibling(0, 1)
    from_sibling(2, 0)
    multiply(core, 3, 2)
    multiply(core, 1, -1)
    multiply(core, 1, 1)
    from_b2(1)
    for d in range(1, 4):
        frm = (z + 4 - d) % 4
        at = pl.ds(pl.multiple_of(core * wh + frm * wq, 16), wq)
        mail.arrived(s_wa[d - 1], wfull.at[at], device(y, frm, core))
    s_ws = mail.slot()
    at = pl.ds(pl.multiple_of(core * wh, 16), wh)
    mail.start(s_ws, wfull.at[at], wfull.at[at], sibling)
    from_b(2)
    from_sibling(0, 2)
    from_sibling(3, 3)
    from_sibling(3, 1)
    multiply(core, 1, 2)
    multiply(core, 2, -1)
    multiply(core, 2, 1)
    from_b2(2)
    from_sibling(3, 2)
    from_sibling(1, 3)
    from_sibling(1, 1)
    from_sibling(1, 2)
    multiply(core, 2, 2)
    from_sibling(2, 3)
    from_sibling(2, 1)
    from_sibling(2, 2)

    mail.arrived(s_ws, wfull.at[pl.ds(pl.multiple_of(other * wh, 16), wh)], sibling)
    width = part.shape[1]
    fold[...] = jnp.where(grp == 0, wfull[:, :width], wfull[:, width:])
    total = jnp.zeros(part.shape, F32)
    for h in range(2):
        a_h = gelu_tanh(pre[h]).astype(BF16)
        act[h] = a_h
        total = total + jnp.dot(
            a_h, fold[h * half : (h + 1) * half], preferred_element_type=F32
        )
    part[...] = total
    mail.arrived(s_nrm, sibt, sibling)
    for ds, dt in NEXT:
        mail.arrived(s_border[ds, dt], borders[ds, dt][1], tile_peer(-ds, -dt))
    mail.finish()


def forward(nrm, nrmt, fc1, fc2, gps, target):
    n_blk, rows, depth = nrm.shape
    hidden = fc2.shape[0]
    half = hidden // 2
    width = gps.shape[2] // 2
    vmem, hbm = pl.BlockSpec(memory_space=VMEM), pl.BlockSpec(memory_space=pl.ANY)
    shape = jax.ShapeDtypeStruct
    return pl.pallas_call(
        forward_kernel,
        out_shape=(
            shape((2, rows, half), F32),
            shape((2, rows, half), BF16),
            shape((rows, width), F32),
            shape((hidden, width), BF16),
            shape(gps.shape[1:], F32),
            shape(nrmt.shape, BF16),
            shape((2, 2) + target.shape[1:], BF16),
            shape((2, target.shape[0], LEAD, target.shape[2]), BF16),
            shape((4, 2, LEAD, target.shape[2]), BF16),
        ),
        in_specs=[vmem, hbm, vmem, vmem, vmem, hbm],
        out_specs=(vmem,) * 5 + (hbm,) * 4,
        scratch_shapes=[
            VMEM((2, n_blk, depth, half), BF16),
            VMEM(gps.shape[1:], F32),
            VMEM((hidden, 2 * width), F32),
            VMEM((half, 2 * width), F32),
            VMEM((half, 2 * width), F32),
            VMEM((half, 2 * width), BF16),
            VMEM((3, half // 4, 2 * width), BF16),
            VMEM((half // 4, 2 * width), BF16),
            VMEM((3, half // 4, 2 * width), BF16),
            VMEM((hidden, 2 * width), BF16),
            pltpu.SemaphoreType.DMA((64,)),
            pltpu.SemaphoreType.DMA((64,)),
        ],
        compiler_params=pltpu.CompilerParams(
            collective_id=1, has_side_effects=True, vmem_limit_bytes=56 * 2**20
        ),
    )(nrm, nrmt, fc1, fc2, gps, target)


def pixel_kernels(lift, conv_a):
    lifted = {
        (o, e): jnp.dot(lift, conv_a[3 * o + e], preferred_element_type=F32)
        for o in range(3)
        for e in range(3)
    }

    def reach(pixel, cell):
        return [o for o in range(3) if (pixel + o - 1) // 2 == cell]

    out = {}
    for r in range(-1, 5):
        for c in range(-1, 5):
            parts = []
            for a in range(2):
                for b in range(2):
                    total = jnp.zeros_like(lifted[0, 0])
                    for o in reach(r, a):
                        for e in reach(c, b):
                            total = total + lifted[o, e]
                    parts.append(total)
            out[r, c] = jnp.concatenate(parts, axis=0)
    return out


def middle_kernel(
    part, xproj, lift, conv_a, conv_b, conv_bt, target, t_rows, t_cols, t_ends,
    latent, lg,
    psrc, main_in, edge_in, patch, kern, f_ref, a_ref, b_ref, acc, want, gf, send, recv,
):
    seq, tile = lax.axis_index("seq"), lax.axis_index("tile")
    greet([tile_peer(ds, dt) for ds, dt in AROUND])
    mail = Courier(send, recv)
    n_rows, n_cols, width = part.shape
    span = main_in.shape[2]
    here = n_cols // 4
    pairs, ch = a_ref.shape[1], a_ref.shape[2] // 4

    psrc[...] = jnp.zeros_like(psrc)
    psrc[:, EDGE : EDGE + n_cols, :] = part[...]
    cols = pl.ds(pl.multiple_of(EDGE + tile * here, 8), here)
    psrc[:, cols, :] = psrc[:, cols, :] + xproj[...]

    def window(dt):
        return pl.ds(pl.multiple_of((tile + dt) % 4 * here, 8), span)

    slots = {}
    for ds, dt in AROUND:
        slots[ds, dt] = mail.slot()
        if ds == 0:
            src, dst = psrc.at[:, window(dt)], main_in.at[dt]
        elif ds == -1:
            src, dst = psrc.at[pl.ds(0, 1), window(dt)], edge_in.at[1, dt]
        else:
            src, dst = psrc.at[pl.ds(n_rows - 1, 1), window(dt)], edge_in.at[0, dt]
        mail.start(slots[ds, dt], src, dst, tile_peer(ds, dt))

    kernels = pixel_kernels(lift[...], conv_a)
    for r in range(-1, 5):
        for c in range(-1, 5):
            kern[6 * (r + 1) + c + 1] = kernels[r, c].astype(BF16)
    height, breadth = target.shape[0], target.shape[1]
    body, lead = slice(LEAD, LEAD + breadth), slice(0, LEAD)
    trail = slice(LEAD + breadth, 2 * LEAD + breadth)
    mid = slice(2, 2 + height)

    def want_at(rows, at, value):
        value = value.astype(F32)
        want[rows, 0, at, :] = value[:, :, :128]
        want[rows, 1, at, :] = value[:, :, 128:]

    want_at(mid, body, target[...])
    want_at(slice(0, 2), body, t_rows[0])
    want_at(slice(2 + height, 4 + height), body, t_rows[1])
    for side, at in ((0, lead), (1, trail)):
        want_at(mid, at, t_cols[side])
        want_at(slice(0, 2), at, t_ends[side])
        want_at(slice(2 + height, 4 + height), at, t_ends[2 + side])

    total = psrc[:, window(0), :]
    for dt in range(1, 4):
        mail.arrived(slots[0, dt], main_in.at[dt], tile_peer(0, -dt))
        total = total + main_in[dt]
    rows = {i + 1: total[i] for i in range(n_rows)}
    for i, ds in ((0, 1), (1, -1)):
        total = jnp.zeros(edge_in.shape[3:], F32)
        for dt in range(4):
            mail.arrived(slots[ds, dt], edge_in.at[i, dt], tile_peer(-ds, -dt))
            total = total + edge_in[i, dt, 0]
        outside = (seq == 0) if i == 0 else (seq == 15)
        rows[0 if i == 0 else n_rows + 1] = jnp.where(outside, 0.0, total)
    n_tok = n_rows + 2
    for r in range(n_tok):
        patch[0, r + 1] = pltpu.roll(rows[r], 1, 0).astype(BF16)
        patch[1, r + 1] = rows[r].astype(BF16)
        patch[2, r + 1] = pltpu.roll(rows[r], span - 1, 0).astype(BF16)
    for k in range(3):
        patch[k, 0] = jnp.zeros((span, width), BF16)
        patch[k, n_tok + 1] = jnp.zeros((span, width), BF16)

    def near(phase):
        return [(d, phase - 4 * d) for d in (-1, 0, 1) if -1 <= phase - 4 * d <= 4]

    for al in range(4):
        for ph in range(4):
            value = None
            for dr, r in near(al):
                for dc, c in near(ph):
                    lhs = patch[1 + dc, 1 + dr : 1 + dr + n_tok].reshape(n_tok * span, width)
                    term = jnp.dot(
                        lhs, kern[6 * (r + 1) + c + 1], preferred_element_type=F32
                    )
                    value = term if value is None else value + term
            value = value.reshape(n_tok, span, ch)
            for tr in range(n_tok):
                at = pl.ds(ph // 2, span, stride=2)
                f_ref[4 * tr + al, ph % 2, 0, at, :] = value[tr, :, :128]
                f_ref[4 * tr + al, ph % 2, 1, at, :] = value[tr, :, 128:]

    def inside(row, b):
        r = seq * height + row
        c = 2 * (tile * breadth // 2 + lax.broadcasted_iota(jnp.int32, (pairs, 1), 0) - EDGE) + b
        return (r >= 0) & (r < 16 * height) & (c >= 0) & (c < 4 * breadth)

    def both(ref, at, rows):
        return jnp.concatenate([ref[*at, 0, rows, :], ref[*at, 1, rows, :]], axis=1)

    def spread(ref, at, v0, v1):
        ref[at, :, 0:ch] = pltpu.roll(v1, 1, 0).astype(BF16)
        ref[at, :, ch : 2 * ch] = v0.astype(BF16)
        ref[at, :, 2 * ch : 3 * ch] = v1.astype(BF16)
        ref[at, :, 3 * ch :] = pltpu.roll(v0, pairs - 1, 0).astype(BF16)

    @pl.loop(0, height + 6)
    def _(i):
        smooth = []
        for b in range(2):
            f = both(f_ref, (i + 1, b), slice(EDGE, EDGE + pairs))
            sigma = jax.nn.sigmoid(f)
            smooth.append(jnp.where(inside(i - 3, b), f * sigma, 0.0))
            slope = sigma * (1.0 + f * (1.0 - sigma))
            f_ref[i + 1, b, 0, EDGE : EDGE + pairs, :] = slope[:, :128]
            f_ref[i + 1, b, 1, EDGE : EDGE + pairs, :] = slope[:, 128:]
        spread(a_ref, i, *smooth)

    def conv(src, weights, out_rows, chunk):
        @pl.loop(0, out_rows // chunk)
        def _(i):
            for b in range(2):
                value = None
                for o in range(3):
                    lhs = src[pl.ds(i * chunk + o, chunk), :, b * ch : (b + 3) * ch]
                    term = jnp.dot(
                        lhs.reshape(chunk * pairs, 3 * ch), weights[o],
                        preferred_element_type=F32,
                    )
                    value = term if value is None else value + term
                acc[b, pl.ds(i * chunk, chunk)] = value.reshape(chunk, pairs, ch)

    conv(a_ref, conv_b, height + 4, (height + 4) // 2)

    @pl.loop(0, height + 4)
    def _(i):
        grad = []
        for b in range(2):
            diff = acc[b, i] - both(want, (i,), pl.ds(b, pairs, stride=2))
            grad.append(jnp.where(inside(i - 2, b), diff, 0.0))
        spread(b_ref, i, *grad)

    conv(b_ref, conv_bt, height + 2, (height + 2) // 2)

    @pl.loop(0, height + 2)
    def _(i):
        for b in range(2):
            value = acc[b, i] * both(f_ref, (i + 3, b), slice(EDGE, EDGE + pairs))
            value = jnp.where(inside(i - 1, b), value, 0.0)
            gf[i, b, 0], gf[i, b, 1] = value[:, :128], value[:, 128:]

    grad = None
    for r in range(-1, 5):
        for c in range(-1, 5):
            at = pl.ds(EDGE + c // 2, here, stride=2)
            lhs = jnp.concatenate(
                [both(gf, (4 * tr + r + 1, c % 2), at).astype(BF16) for tr in range(n_rows)],
                axis=0,
            )
            term = lax.dot_general(
                lhs, kern[6 * (r + 1) + c + 1], (((1,), (1,)), ((), ())),
                preferred_element_type=F32,
            )
            grad = term if grad is None else grad + term
    grad = grad.reshape(n_rows, here, width)
    latent[...] = grad
    own = pl.ds(pl.multiple_of(tile * here, 16), here)
    lg[:, own, :] = grad.astype(BF16)
    back = [mail.slot() for _ in range(3)]
    for dt in range(1, 4):
        mail.start(back[dt - 1], lg.at[:, own], lg.at[:, own], tile_peer(0, dt))
    for dt in range(1, 4):
        frm = pl.ds(pl.multiple_of((tile + 4 - dt) % 4 * here, 16), here)
        mail.arrived(back[dt - 1], lg.at[:, frm], tile_peer(0, -dt))
    mail.finish()


def middle(part, xproj, lift, conv_a, conv_b, conv_bt, target, t_rows, t_cols, t_ends):
    n_rows, n_cols, width = part.shape
    height, breadth, ch = target.shape
    here, span = n_cols // 4, n_cols // 4 + 2 * EDGE
    pairs = breadth // 2 + 2 * EDGE
    vmem = pl.BlockSpec(memory_space=VMEM)
    shape = jax.ShapeDtypeStruct
    return pl.pallas_call(
        middle_kernel,
        out_shape=(
            shape((n_rows, here, width), F32),
            shape((n_rows, n_cols, width), BF16),
        ),
        in_specs=[vmem] * 10,
        out_specs=(vmem,) * 2,
        scratch_shapes=[
            VMEM((n_rows, n_cols + 2 * EDGE, width), F32),
            VMEM((4, n_rows, span, width), F32),
            VMEM((2, 4, 1, span, width), F32),
            VMEM((3, n_rows + 4, span, width), BF16),
            VMEM((36, width, ch), BF16),
            VMEM((height + 8, 2, 2, 2 * span, ch // 2), F32),
            VMEM((height + 6, pairs, 4 * ch), BF16),
            VMEM((height + 4, pairs, 4 * ch), BF16),
            VMEM((2, height + 4, pairs, ch), F32),
            VMEM((height + 4, 2, breadth + 2 * LEAD, ch // 2), F32),
            VMEM((height + 2, 2, 2, pairs, ch // 2), F32),
            pltpu.SemaphoreType.DMA((16,)),
            pltpu.SemaphoreType.DMA((16,)),
        ],
        compiler_params=pltpu.CompilerParams(
            collective_id=3, has_side_effects=True, vmem_limit_bytes=56 * 2**20
        ),
    )(part, xproj, lift, conv_a, conv_b, conv_bt, target, t_rows, t_cols, t_ends)


def gelu_slope(x):
    k = 0.7978845608028654
    t = jnp.tanh(k * (x + 0.044715 * x * x * x))
    return 0.5 * (1.0 + t) + 0.5 * x * (1.0 - t * t) * (k + 3 * 0.044715 * k * x * x)


def backward_kernel(
    nrmt, sibt, pre, act, fold, lg, out, sfull,
    gpre, gsib, st, ssib, ssum, sz_in, sy_out, sy_in,
    far_out, up_out, down_out, half_in, full_in, reduced, fin, send, recv,
):
    y, z, core, device = place()
    a, b, turn = oriented(y, z, core)
    grp = lax.axis_index("grp")
    other = 1 - core
    sibling = device(y, z, other)
    greet(plane_peers(y, z, core, device))
    mail = Courier(send, recv)
    depth, half = gpre.shape[1], gpre.shape[2]
    rows = nrmt.shape[1] // 2
    top, bottom = pl.ds(0, rows), pl.ds(rows, rows)

    def peer(da, db):
        return device(*turn((a + da) % 4, (b + db) % 4), core)

    def block(da, db):
        return block_of(*turn((a + da) % 4, (b + db) % 4))

    def pre_grad(h):
        weights = fold[pl.ds(pl.multiple_of(h * half, 16), half), :]
        grad_act = lax.dot_general(
            lg[...], weights, (((1,), (1,)), ((), ())), preferred_element_type=F32
        )
        gpre[h] = (grad_act * gelu_slope(pre[h])).astype(BF16)

    s_g = mail.slot()
    pre_grad(other)
    mail.start(s_g, gpre.at[other], gsib, sibling)
    pre_grad(core)
    for h in range(2):
        st[:, h * half : (h + 1) * half] = lax.dot_general(
            lg[...], act[h], (((0,), (0,)), ((), ())), preferred_element_type=F32
        )
    sr = st.shape[0] // 2
    sq = sr // 4
    s_s = mail.slot()
    mail.start(s_s, st.at[pl.ds(pl.multiple_of(other * sr, 8), sr)], ssib, sibling)

    mail.arrived(s_g, gsib, sibling)

    def term(da, db):
        at = block(da, db)
        return jnp.dot(nrmt[at], gpre[core], preferred_element_type=F32) + jnp.dot(
            sibt[at], gsib[...], preferred_element_type=F32
        )

    def far(i, value, to):
        s = [mail.slot() for _ in range(2)]
        far_out[i] = value.astype(BF16)
        mail.start(s[0], far_out.at[i, top], half_in.at[i, 0], to(1))
        mail.start(s[1], far_out.at[i, bottom], half_in.at[i, 1], to(-1))
        return s

    def near(i, up, down, to, s_far):
        s = [mail.slot() for _ in range(2)]
        mail.arrived(s_far[0], half_in.at[i, 0], to(-1))
        up_out[i, :rows] = (up[:rows] + half_in[i, 0].astype(F32)).astype(BF16)
        up_out[i, rows:] = up[rows:].astype(BF16)
        mail.start(s[0], up_out.at[i], full_in.at[i, 0], to(1))
        mail.arrived(s_far[1], half_in.at[i, 1], to(1))
        down_out[i, :rows] = down[:rows].astype(BF16)
        down_out[i, rows:] = (down[rows:] + half_in[i, 1].astype(F32)).astype(BF16)
        mail.start(s[1], down_out.at[i], full_in.at[i, 1], to(-1))
        return s

    def last(i, own, to, s_near):
        mail.arrived(s_near[0], full_in.at[i, 0], to(-1))
        mail.arrived(s_near[1], full_in.at[i, 1], to(1))
        return own + full_in[i, 0].astype(F32) + full_in[i, 1].astype(F32)

    def along_a(d):
        return peer(d, 0)

    def along_b(d):
        return peer(0, d)

    def b_far(da):
        return far(da, term(da, 2), along_b)

    def b_near(da, s):
        return near(da, term(da, 1), term(da, -1), along_b, s)

    def b_last(da, s):
        reduced[da] = last(da, term(da, 0), along_b, s)

    f2 = b_far(2)
    f3 = b_far(3)
    n2 = b_near(2, f2)

    mail.arrived(s_s, ssib, sibling)
    ssum[...] = st[pl.ds(pl.multiple_of(core * sr, 8), sr), :] + ssib[...]
    s_sz = [mail.slot() for _ in range(3)]
    for d in range(1, 4):
        to = (z + d) % 4
        src = ssum.at[pl.ds(pl.multiple_of(to * sq, 8), sq)]
        mail.start(s_sz[d - 1], src, sz_in.at[d - 1], device(y, to, core))

    f1 = b_far(1)
    n3 = b_near(3, f3)
    b_last(2, n2)
    fa = far(4, reduced[2], along_a)

    for d in range(1, 4):
        mail.arrived(s_sz[d - 1], sz_in.at[d - 1], device(y, (z + 4 - d) % 4, core))
    total = ssum[pl.ds(pl.multiple_of(z * sq, 8), sq), :] + sz_in[0] + sz_in[1] + sz_in[2]
    sy_out[...] = total
    s_sy = [mail.slot() for _ in range(3)]
    for d in range(1, 4):
        mail.start(s_sy[d - 1], sy_out, sy_in.at[d - 1], device((y + d) % 4, z, core))

    f0 = b_far(0)
    n1 = b_near(1, f1)
    b_last(3, n3)

    for d in range(1, 4):
        mail.arrived(s_sy[d - 1], sy_in.at[d - 1], device((y + 4 - d) % 4, z, core))
    s_at = pl.ds(pl.multiple_of(core * sr + z * sq, 8), sq)
    sfull[grp, s_at] = sy_out[...] + sy_in[1]
    sfull[1 - grp, s_at] = sy_in[0] + sy_in[2]
    s_sa = [mail.slot() for _ in range(3)]
    for d in range(1, 4):
        mail.start(
            s_sa[d - 1], sfull.at[:, s_at], sfull.at[:, s_at], device(y, (z + d) % 4, core)
        )

    n0 = b_near(0, f0)
    b_last(1, n1)
    na = near(4, reduced[1], reduced[3], along_a, fa)
    b_last(0, n0)

    for d in range(1, 4):
        frm = (z + 4 - d) % 4
        at = pl.ds(pl.multiple_of(core * sr + frm * sq, 8), sq)
        mail.arrived(s_sa[d - 1], sfull.at[:, at], device(y, frm, core))
    s_ss = mail.slot()
    at = pl.ds(pl.multiple_of(core * sr, 8), sr)
    mail.start(s_ss, sfull.at[:, at], sfull.at[:, at], sibling)

    fin[...] = last(4, reduced[0], along_a, na)
    s_fin = mail.slot()
    theirs = pl.ds(pl.multiple_of(other * rows, 16), rows)
    mail.start(s_fin, fin.at[theirs], out.at[core], sibling)
    out[core] = fin[pl.ds(pl.multiple_of(core * rows, 16), rows), :]
    at = pl.ds(pl.multiple_of(other * sr, 8), sr)
    mail.arrived(s_ss, sfull.at[:, at], sibling)
    mail.arrived(s_fin, out.at[other], sibling)
    mail.finish()


def backward(nrmt, sibt, pre, act, fold, lg):
    n_blk, depth, rows = nrmt.shape
    half = pre.shape[2]
    width = lg.shape[1]
    vmem = pl.BlockSpec(memory_space=VMEM)
    shape = jax.ShapeDtypeStruct
    return pl.pallas_call(
        backward_kernel,
        out_shape=(shape((2, depth // 2, half), F32), shape((2, width, 2 * half), F32)),
        in_specs=[vmem] * 6,
        out_specs=(vmem,) * 2,
        scratch_shapes=[
            VMEM((2, rows, half), BF16),
            VMEM((rows, half), BF16),
            VMEM((width, 2 * half), F32),
            VMEM((width // 2, 2 * half), F32),
            VMEM((width // 2, 2 * half), F32),
            VMEM((3, width // 8, 2 * half), F32),
            VMEM((width // 8, 2 * half), F32),
            VMEM((3, width // 8, 2 * half), F32),
            VMEM((5, depth, half), BF16),
            VMEM((5, depth, half), BF16),
            VMEM((5, depth, half), BF16),
            VMEM((5, 2, depth // 2, half), BF16),
            VMEM((5, 2, depth, half), BF16),
            VMEM((4, depth, half), F32),
            VMEM((depth, half), F32),
            pltpu.SemaphoreType.DMA((40,)),
            pltpu.SemaphoreType.DMA((40,)),
        ],
        compiler_params=pltpu.CompilerParams(
            collective_id=2, has_side_effects=True, vmem_limit_bytes=56 * 2**20
        ),
    )(nrmt, sibt, pre, act, fold, lg)


def shards(tokens, shift, scale, gate, fc1, fc2, proj, lift, conv_a, conv_b, target):
    tok_here, tok_cols, width = (tokens.shape[1], tokens.shape[2], tokens.shape[3])
    n_seq, n_tile = lax.axis_size("seq"), lax.axis_size("tile")
    seq, tile, grp = lax.axis_index("seq"), lax.axis_index("tile"), lax.axis_index("grp")
    rows_x = tokens[0].reshape(-1, width)
    proj_full = proj.astype(F32)
    patch_width = proj.shape[1]

    cols_here = fc2.shape[1]
    gps = []
    for at in (grp, 1 - grp):
        col_at = (at * n_seq + seq) * cols_here
        gate_cols = lax.dynamic_slice_in_dim(gate[0], col_at, cols_here, 0)
        proj_cols = lax.dynamic_slice_in_dim(proj_full, col_at, cols_here, 0)
        here = gate_cols[:, None] * proj_cols
        zero = jnp.zeros_like(here)
        first_image = jnp.concatenate([here, zero], axis=1)
        gps.append(jnp.where(grp == 0, first_image, jnp.roll(first_image, patch_width, axis=1)))
    gps = jnp.pad(jnp.stack(gps), ((0, 0), (0, 4), (0, 0)))

    xfull = rows_x.astype(F32)
    center = xfull - jnp.mean(xfull, axis=1, keepdims=True)
    spread = jnp.mean(center * center, axis=1, keepdims=True)
    normed = (center * lax.rsqrt(spread + 1e-06) * (1.0 + scale[0]) + shift[0]).astype(BF16)
    nrm = jnp.pad(normed.reshape(-1, 2 * n_seq, cols_here), ((0, 0), (0, 0), (0, 4)))
    nrm = nrm.reshape(-1, n_seq, 2 * (cols_here + 4)).transpose(1, 0, 2)
    nrmt = nrm.transpose(0, 2, 1)
    pre, act, partial, folded, gated, sibt, *borders = forward(
        nrm,
        nrmt,
        jnp.pad(fc1, ((0, 4), (0, 0))),
        jnp.pad(fc2, ((0, 0), (0, 4))),
        gps,
        target[0],
    )
    col_count = tok_cols // n_tile
    x_mine = lax.dynamic_slice_in_dim(tokens[0], tile * col_count, col_count, 1)
    xproj = jnp.dot(x_mine, proj, preferred_element_type=F32)
    ch = conv_a.shape[2]
    conv_bt = jnp.swapaxes(conv_b[::-1, ::-1], 2, 3).reshape(3, 3 * ch, ch)
    latent_mine, latent_rows = middle(
        partial.reshape(tok_here, tok_cols, patch_width),
        xproj,
        lift,
        conv_a.reshape(9, ch, ch),
        conv_b.reshape(3, 3 * ch, ch),
        conv_bt,
        target[0],
        *borders,
    )
    latent_rows = latent_rows.reshape(-1, patch_width)
    grad_one, outers = backward(nrmt, sibt, pre, act, folded, latent_rows)
    grad_one = grad_one.transpose(1, 0, 2).reshape(grad_one.shape[1], -1)[:cols_here]
    grad_two = lax.dot_general(
        outers.reshape(2 * patch_width, -1),
        gated[:cols_here],
        (((0,), (1,)), ((), ())),
        precision=lax.Precision.HIGHEST,
    )
    return (grad_one, grad_two, latent_mine[None])


def solution(mesh):
    in_specs = (
        P("grp", "seq", None, None),
        P("grp", None),
        P("grp", None),
        P("grp", None),
        P(("grp", "seq"), "tile"),
        P("tile", ("grp", "seq")),
        P(),
        P(),
        P(),
        P(),
        P("grp", "seq", "tile", None),
    )
    out_specs = (
        P(("grp", "seq"), "tile"),
        P("tile", ("grp", "seq")),
        P("grp", "seq", "tile", None),
    )
    return jax.shard_map(shards, mesh=mesh, in_specs=in_specs, out_specs=out_specs, check_vma=False)
```

time: 497 us -> 160 us (0.32); the launches traced: 487 us -> 160 us
  waiting for transfers between devices: 301 us -> 0 us
  Pallas kernels: 0 us -> 125 us
  matrix products: 56.3 us -> 4.45 us
  starting transfers between devices: 40.4 us -> 0 us
  other arithmetic: 26.3 us -> 5.2 us
  between operations: 15.3 us -> 0.85 us
  local copies, waits for them, and re-layouts: 38.3 us -> 24.1 us
  blocking collectives: 9.34 us -> 0 us
    unnamed x5 -> x0, waiting for transfers between devices: 135 us -> none
    pallas_call x0 -> x3, Pallas kernels: none -> 125 us  [the longest x1 51.3 us: forward(): pl.pallas_call(forward_kernel, out_shape=(shape((2, rows, half), F32), sh...]
    all_gather x2 -> x0, waiting for transfers between devices: 104 us -> none  [the longest x1 55.8 us: shards(): lax.all_gather(fc1, ('grp', 'seq'), axis=0, tiled=True)]
    dot_general x46 -> x2, matrix products: 56.3 us -> 4.45 us  [the longest x1 2.42 us: shards(): lax.dot_general(outers.reshape(2 * patch_width, -1), gated[:cols_here], (...]
    ppermute x16 -> x0, starting transfers between devices: 40.3 us -> none  [the longest x8 27.2 us: padded_2(): before = lax.ppermute(last, axis, up)]
    psum x1 -> x0, waiting for transfers between devices: 35.7 us -> none  [shards(): lax.psum(partial_value.astype(jnp.bfloat16), 'tile').astype(jnp.float32)]
    ppermute x16 -> x0, waiting for transfers between devices: 27 us -> none  [the longest x8 27 us: padded_2(): after = lax.ppermute(leading, axis, down)]
    unnamed x34 -> x25, local copies, waits for them, and re-layouts: 26.2 us -> 3.11 us
  transfers between devices with their start and end apart: 20 -> 0, of which waited for: 12 -> 0; matrix products, arithmetic and copies ran while one was open for 8% -> 0% of each run, Pallas kernels for 0% -> 0%
where the time goes in v1:
time: 160 us
  Pallas kernels  125 us (78%)
  local copies, waits for them, and re-layouts  24.1 us (15%)
  other arithmetic  5.2 us (3%)
  matrix products  4.45 us (3%)
    pallas_call x1, Pallas kernels, forward(): pl.pallas_call(forward_kernel, out_shape=(shape((2, rows, half), F32), sh...  51.3 us
    pallas_call x1, Pallas kernels, backward(): pl.pallas_call(backward_kernel, out_shape=(shape((2, depth // 2, half), F...  40.1 us
    pallas_call x1, Pallas kernels, middle(): pl.pallas_call(middle_kernel, out_shape=(shape((n_rows, here, width), F32...  33.9 us
    convert_element_type x2, local copies, waits for them, and re-layouts, shards(): xfull = rows_x.astype(F32)  10.6 us
    transpose x1, local copies, waits for them, and re-layouts, shards(): nrm = nrm.reshape(-1, n_seq, 2 * (cols_here + 4)).transpose(1, 0, 2)  4.55 us

profile of v1, /device:TPU:1, one launch (start us, length us, event | category | flops | bytes accessed | tf_op | source)
XLA Modules:
  0.0 160.0 jit_solution(1907668918317021450)
XLA Ops:
  0.6 0.0 copy-start.1
  0.7 0.9 fusion.7
  1.6 1.3 copy.21
  2.9 0.1 convert_element_type.30
  3.0 0.1 dynamic-slice_multiply_fusion.1
  3.1 0.1 select_bitcast_fusion
  3.2 0.6 select_maximum_fusion.gps
  3.8 0.0 copy-done.1
  3.8 0.4 convert_reduce_fusion
  4.2 0.8 multiply_reduce_fusion
  5.0 3.7 %copy.19 = f32[1,4,128,2432]{2,1,3,0:T(4,128)} copy(bf16[1,4,128,2432]{3,2,1,0:T(8,128)(2,1)S(1)} %copy-done.1) | data formatting | bytes 7471104 | tf_op jit(solution)/shard_map/convert_element_type | solution.py:835
  8.8 0.0 copy-start.8
  8.8 0.0 copy-start.9
  8.8 6.9 %reshape.101 = f32[512,32,76]{0,2,1:T(8,128)} reshape(f32[1,4,128,2432]{2,1,3,0:T(4,128)} %copy.19) | data formatting | bytes 9961472 | tf_op jit(solution)/shard_map/convert_element_type | solution.py:835
  15.6 0.0 copy-done.8
  15.7 0.1 add.67
  15.8 0.0 copy-done.9
  15.8 0.1 mul.62
  15.9 3.0 %add_convert_fusion = bf16[512,32,76]{0,2,1:T(8,128)(2,1)S(1)} fusion(f32[512,32,76]{0,2,1:T(8,128)} %reshape.101, f32[32,76]{1,0:T(8,128)S(1)} %add.67, f32[32,76]{1,0:T(8,128)S(1)} %mul.62, f32[512]{0:T(512)S(1)} %rsqrt_bitcast_fusion, f32[512]{0:T(512)S(1)} %get-tuple-element.33), kind=kLoop, calls=%fused_computation | loop fusion | flops 6225920 | bytes 7494656 | tf_op jit(solution)/shard_map/convert_element_type | solution.py:838
  19.0 0.2 pad.20
  19.2 0.0 copy-start
  19.2 0.0 copy-start.5
  19.2 0.0 copy-start.4
  19.3 4.5 %copy.22.nrm = bf16[16,512,160]{2,1,0:T(8,128)(2,1)} copy(bf16[16,512,160]{1,2,0:T(8,128)(2,1)S(1)} %bitcast.41) | data formatting | bytes 5242880 | tf_op jit(solution)/shard_map/transpose | solution.py:840
  23.8 0.0 copy-done
  23.8 0.0 copy-done.5
  23.8 0.2 copy.20
  24.0 0.8 pad.22.fc2
  24.8 0.0 copy-done.4
  24.8 0.7 pad.21.fc1
  25.5 0.0 copy-start.3
  25.5 0.0 copy-start.2
  25.5 51.3 %shard_map.130 = (f32[2,512,640]{2,1,0:T(8,128)}, bf16[2,512,640]{2,1,0:T(8,128)(2,1)}, f32[512,64]{1,0:T(8,128)}, bf16[1280,64]{1,0:T(8,128)(2,1)}, f32[80,128]...) custom-call(bf16[16,512,160]{2,1,0:T(8,128)(2,1)} %copy.22.nrm, ...), custom_call_target="tpu_custom_call" | custom-call | tf_op jit(solution)/shard_map/pallas_call | solution.py:345
  76.9 0.0 copy-done.3
  76.9 2.0 %fusion.xproj = f32[4,32,64]{2,1,0:T(8,128)} fusion(bf16[1,4,128,2432]{3,2,1,0:T(8,128)(2,1)} %param.11, s32[]{:T(128)S(6)} %select_n.28, bf16[2432,64]{0,1:T(8,128)(2,1)S(1)} %copy-done.3), kind=kOutput, calls=%fused_computation.4 | convolution fusion | flops 39845888 | bytes 966660 | tf_op jit(solution)/shard_map/dot_general | solution.py:852
  78.9 0.0 copy-done.2
  78.9 0.1 reverse_bitcast_fusion
  79.0 1.7 %copy.23 = bf16[3,3,256,256]{3,2,1,0:T(8,128)(2,1)} copy(bf16[3,3,256,256]{2,3,1,0:T(8,128)(2,1)S(1)} %reverse_bitcast_fusion) | data formatting | bytes 2359296 | tf_op jit(solution)/shard_map/transpose | solution.py:854
  80.8 33.9 %shard_map.131 = (f32[4,32,64]{2,1,0:T(8,128)}, bf16[4,128,64]{2,1,0:T(8,128)(2,1)}) custom-call(f32[4,128,64]{2,1,0:T(8,128)} %bitcast.53, f32[4,32,64]{2,1,0:T(8,128)} %fusion.xproj, bf16[16,256]{1,0:T(8,128)(2,1)} %lift.1, bf16[9,256,256]{2,1,0:T(8,128)(2,1)} %bitcast.49, bf16[3,768,256]{2,1,0:T(8,128)(2,1)} %bitcast.44, bf16[3,768,256]{2,1,0:T(8,128)(2,1)} %bitcast.45, ...), custom_call_target="tpu_custom_call" | custom-call | tf_op jit(solution)/shard_map/pallas_call | solution.py:591
  114.7 0.0 copy-start.7
  114.7 40.1 %shard_map.132 = (f32[2,80,640]{2,1,0:T(8,128)}, f32[2,64,1280]{2,1,0:T(8,128)}) custom-call(bf16[16,160,512]{2,1,0:T(8,128)(2,1)} %bitcast.43, bf16[16,160,512]{2,1,0:T(8,128)(2,1)} %get-tuple-element.16.sibt, f32[2,512,640]{2,1,0:T(8,128)} %get-tuple-element.17.pre, bf16[2,512,640]{2,1,0:T(8,128)(2,1)} %get-tuple-element.18.act, ...), custom_call_target="tpu_custom_call" | custom-call | tf_op jit(solution)/shard_map/pallas_call | solution.py:785
  154.8 0.0 copy-start.6
  154.8 0.0 copy-done.7
  154.8 2.4 %fusion.4 = f32[1280,76]{0,1:T(8,128)} fusion(f32[128,1280]{1,0:T(8,128)} %bitcast.50, f32[80,128]{1,0:T(8,128)S(1)} %copy-done.7), kind=kOutput, calls=%fused_computation.10 | convolution fusion | flops 149422080 | bytes 1085440 | tf_op jit(solution)/shard_map/dot_general | solution.py:868
  157.2 1.2 copy.24
  158.5 0.1 pad.28
  158.6 0.8 copy.25
  159.4 0.0 copy-done.6
  159.4 0.6 copy.27
  (4 shorter events, 0.1 us)
Async XLA Ops:
  0.6 3.2 %copy-start.1 = (bf16[1,4,128,2432]{3,2,1,0:T(8,128)(2,1)S(1)}, bf16[1,4,128,2432]{3,2,1,0:T(8,128)(2,1)}, u32[]{:S(2)}) copy-start(bf16[1,4,128,2432]{3,2,1,0:T(8,128)(2,1)} %param.11) | copy-start | bytes 7471108
  8.8 6.9 %copy-start.8 = (f32[1,2432]{1,0:T(1,128)S(1)}, f32[1,2432]{1,0:T(1,128)}, u32[]{:S(2)}) copy-start(f32[1,2432]{1,0:T(1,128)} %param.12) | copy-start | bytes 29188
  8.8 7.0 %copy-start.9 = (f32[1,2432]{1,0:T(1,128)S(1)}, f32[1,2432]{1,0:T(1,128)}, u32[]{:S(2)}) copy-start(f32[1,2432]{1,0:T(1,128)} %param.13) | copy-start | bytes 29188
  19.2 4.6 %copy-start = (bf16[512,32,80]{0,2,1:T(8,128)(2,1)}, bf16[512,32,80]{0,2,1:T(8,128)(2,1)S(1)}, u32[]{:S(2)}) copy-start(bf16[512,32,80]{0,2,1:T(8,128)(2,1)S(1)} %pad.20) | copy-start | bytes 7864324
  19.2 4.6 %copy-start.5 = (bf16[1280,76]{0,1:T(8,128)(2,1)S(1)}, bf16[1280,76]{0,1:T(8,128)(2,1)}, u32[]{:S(2)}) copy-start(bf16[1280,76]{0,1:T(8,128)(2,1)} %param.16) | copy-start | bytes 583684
  19.2 5.6 %copy-start.4 = (bf16[76,1280]{1,0:T(8,128)(2,1)S(1)}, bf16[76,1280]{1,0:T(8,128)(2,1)}, u32[]{:S(2)}) copy-start(bf16[76,1280]{1,0:T(8,128)(2,1)} %param.15) | copy-start | bytes 583684
  25.5 51.4 %copy-start.3 = (bf16[2432,64]{0,1:T(8,128)(2,1)S(1)}, bf16[2432,64]{0,1:T(8,128)(2,1)}, u32[]{:S(2)}) copy-start(bf16[2432,64]{0,1:T(8,128)(2,1)} %param.17) | copy-start | bytes 933892
  25.5 53.4 %copy-start.2 = (bf16[3,3,256,256]{3,2,1,0:T(8,128)(2,1)S(1)}, bf16[3,3,256,256]{3,2,1,0:T(8,128)(2,1)}, u32[]{:S(2)}) copy-start(bf16[3,3,256,256]{3,2,1,0:T(8,128)(2,1)} %param.20) | copy-start | bytes 3538948
  114.7 40.1 %copy-start.7 = (f32[80,128]{1,0:T(8,128)S(1)}, f32[80,128]{1,0:T(8,128)}, u32[]{:S(2)}) copy-start(f32[80,128]{1,0:T(8,128)} %get-tuple-element.27) | copy-start | bytes 122884
  154.8 4.6 %copy-start.6 = (f32[4,32,64]{2,1,0:T(8,128)S(1)}, f32[4,32,64]{2,1,0:T(8,128)}, u32[]{:S(2)}) copy-start(f32[4,32,64]{2,1,0:T(8,128)} %get-tuple-element.28) | copy-start | bytes 98308

commit v2 on v0

v2 whole, which is shorter than its diff:
```python
import jax
import jax.numpy as jnp
from jax import lax
from jax.experimental import pallas as pl
from jax.experimental.pallas import tpu as pltpu
from jax.sharding import PartitionSpec as P

F32 = jnp.float32
BF16 = jnp.bfloat16
MESH = pl.DeviceIdType.MESH
VMEM = pltpu.VMEM
NT = (((1,), (1,)), ((), ()))
TN = (((0,), (0,)), ((), ()))
EDGE = 8
LEAD = 16
NEXT = [(1, 0), (-1, 0), (0, 1), (0, -1), (1, 1), (1, -1), (-1, 1), (-1, -1)]
AROUND = [(0, 1), (0, 2), (0, 3)] + [(ds, dt) for ds in (-1, 1) for dt in range(4)]
STEPS = (1, 3, 2)


def gelu_tanh(value):
    return jax.nn.gelu(value, approximate=True)


def gelu_slope(x):
    k = 0.7978845608028654
    t = jnp.tanh(k * (x + 0.044715 * x * x * x))
    return 0.5 * (1.0 + t) + 0.5 * x * (1.0 - t * t) * (k + 3 * 0.044715 * k * x * x)


def split(value):
    high = value.astype(BF16)
    return high, (value - high.astype(F32)).astype(BF16)


def dot(lhs, rhs, dims=(((1,), (0,)), ((), ()))):
    return lax.dot_general(lhs, rhs, dims, preferred_element_type=F32)


def place():
    grp, seq, tile = lax.axis_index("grp"), lax.axis_index("seq"), lax.axis_index("tile")
    core = seq % 2
    y = (seq // 2) % 2 * 2 + grp
    z = seq // 4

    def device(y, z, core):
        return (y % 2, z * 4 + y // 2 * 2 + core, tile)

    return y, z, core, device


def oriented(y, z, core):
    a = y + core * (z - y)
    b = z + core * (y - z)

    def turn(a, b):
        return a + core * (b - a), b + core * (a - b)

    return a, b, turn


def block_of(y, z):
    return y % 2 * 8 + z * 2 + y // 2


def tile_peer(ds, dt):
    grp, seq, tile = lax.axis_index("grp"), lax.axis_index("seq"), lax.axis_index("tile")
    return (grp, (seq + ds) % 16, (tile + dt) % 4)


def announce(peers):
    for peer in peers:
        pl.semaphore_signal(
            pltpu.get_barrier_semaphore(), inc=1, device_id=peer, device_id_type=MESH
        )


def await_peers(peers):
    pl.semaphore_wait(pltpu.get_barrier_semaphore(), len(peers))


def greet(peers):
    announce(peers)
    await_peers(peers)


class Courier:
    def __init__(self, send, recv):
        self.send, self.recv, self.used, self.started = send, recv, 0, []

    def slot(self, count=1):
        self.used += count
        return self.used - count

    def slots(self, keys):
        return {key: self.slot() for key in keys}

    def copy(self, slot, src, dst, peer, landing=None):
        return pltpu.make_async_remote_copy(
            src_ref=src,
            dst_ref=dst,
            send_sem=self.send.at[slot],
            recv_sem=self.recv.at[slot if landing is None else landing],
            device_id=peer,
            device_id_type=MESH,
        )

    def start(self, slot, src, dst, peer, landing=None):
        copy = self.copy(slot, src, dst, peer, landing)
        copy.start()
        self.started.append(copy)

    def arrived(self, slot, dst, peer):
        self.copy(slot, dst, dst, peer).wait_recv()

    def finish(self):
        for copy in self.started:
            copy.wait_send()


def forward_kernel(
    tokens, shift, scale, proj, fc1, fc2, gps, target,
    slope_hbm, act_hbm, sums, fold, gboth, nrmt_hbm, t_rows, t_cols, t_ends,
    normed, nrm, nrmt, gath, gin, wpart, wsib, wsum, wz_out, wz_in, wy_out, wy_in, wfull, xp,
    pre, act, part, part_in, psrc, main_in, edge_in, send, recv, local,
):
    y, z, core, device = place()
    a, b, turn = oriented(y, z, core)
    grp, tile = lax.axis_index("grp"), lax.axis_index("tile")
    other = 1 - core
    sibling = device(y, z, other)
    greet(
        [sibling]
        + [device((y + d) % 4, z, k) for d in STEPS for k in range(2)]
        + [device(y, (z + d) % 4, k) for d in STEPS for k in range(2)]
        + [tile_peer(ds, dt) for ds, dt in AROUND]
    )
    mail = Courier(send, recv)
    rows, half = gath.shape[1] // 2, gath.shape[2]
    here_rows, width = tokens.shape

    def peer(da, db):
        return device(*turn((a + da) % 4, (b + db) % 4), core)

    def block(da, db):
        return block_of(*turn((a + da) % 4, (b + db) % 4))

    own = block(0, 0)
    mine = pl.ds(pl.multiple_of(core * rows, 16), rows)
    theirs = pl.ds(pl.multiple_of(other * rows, 16), rows)
    s_a = mail.slots((h, d) for h in range(2) for d in STEPS)
    r_a = {d: mail.slot(2) for d in STEPS}
    s_gate, s_own = mail.slot(), mail.slot()
    partner = device(y // 2 * 2 + 1 - grp, z, core)
    mail.start(s_gate, gps.at[1], gin, partner)
    src = fc1.at[:, pl.ds(pl.multiple_of(other * half, 128), half)]
    mail.start(s_own, src, gath.at[own, mine], sibling)
    for d in STEPS:
        for h in range(2):
            to = device((y + d) % 4, z, 0) if h == 0 else device(y, (z + d) % 4, 1)
            src = fc1.at[:, h * half : (h + 1) * half]
            mail.start(s_a[h, d], src, gath.at[own, mine], to, r_a[d] + core)
    gath[own, mine, :] = fc1[:, pl.ds(pl.multiple_of(core * half, 128), half)]

    @pl.loop(0, here_rows // 64)
    def _(i):
        at = pl.ds(pl.multiple_of(i * 64, 64), 64)
        x = tokens[at, :].astype(F32)
        center = x - jnp.mean(x, axis=1, keepdims=True)
        spread = jnp.mean(center * center, axis=1, keepdims=True)
        value = center * lax.rsqrt(spread + 1e-06) * (1.0 + scale[...]) + shift[...]
        normed[at, :] = value.astype(BF16)

    mail.arrived(s_gate, gin, partner)
    both = gps[0] + gin[...]
    gboth[...] = both
    high, low = split(both[: fc2.shape[1]])
    wpart[...] = dot(fc2[...], high) + dot(fc2[...], low)
    wq = half // 4
    s_w = mail.slot()
    mail.start(s_w, wpart.at[pl.ds(pl.multiple_of(other * half, 16), half)], wsib, sibling)

    blk_rows = pl.ds(pl.multiple_of(core * here_rows, 128), here_rows)
    cols = fc2.shape[1]

    def rechunk(i):
        first = 2 * cols * i // 128 * 128
        off = 2 * cols * i - first
        span = 256 if off + 2 * cols <= 256 else 384
        r = lax.broadcasted_iota(jnp.int32, (2 * rows, span), 0)
        k = lax.broadcasted_iota(jnp.int32, (2 * rows, span), 1)
        low_part = (k == r + off) & (r < cols)
        high_part = (k == r + (off + cols - rows)) & (r >= rows) & (r < rows + cols)
        pick = jnp.where(low_part | high_part, 1.0, 0.0).astype(BF16)
        value = normed[:, first : first + span]
        nrm[i, blk_rows, :] = dot(value, pick, NT).astype(BF16)
        nrmt[i, :, blk_rows] = dot(pick, value, NT).astype(BF16)

    s_n = mail.slots((q, k) for q in range(4) for k in range(2))

    def rechunk_four(q):
        for i in range(4 * q, 4 * q + 4):
            rechunk(i)
        four = pl.ds(4 * q, 4)
        ref = nrm.at[four, blk_rows]
        mail.start(s_n[q, 0], ref, ref, sibling)
        ref = nrmt.at[four, :, blk_rows]
        mail.start(s_n[q, 1], ref, ref, sibling)

    mail.arrived(s_w, wsib, sibling)
    wsum[...] = wpart[pl.ds(pl.multiple_of(core * half, 16), half), :] + wsib[...]
    wz_out[...] = wsum[...].astype(BF16)
    s_wz, s_wy, s_wa = mail.slots(STEPS), mail.slots(STEPS), mail.slots(STEPS)
    for d in STEPS:
        to = (z + d) % 4
        src = wz_out.at[pl.ds(pl.multiple_of(to * wq, 16), wq)]
        mail.start(s_wz[d], src, wz_in.at[d - 1], device(y, to, core))

    s_b = mail.slots((da, d) for da in range(4) for d in STEPS)

    def put_b(da):
        ref = gath.at[block(da, 0)]
        for d in STEPS:
            mail.start(s_b[da, d], ref, ref, peer(0, d))

    mail.arrived(s_own, gath.at[own, theirs], sibling)
    put_b(0)
    rechunk_four(0)

    def relay(d):
        at = block(-d, 0)
        frm = turn((a + 4 - d) % 4, b)
        for k in range(2):
            landed = gath.at[at, pl.ds(k * rows, rows)]
            mail.arrived(r_a[d] + k, landed, device(*frm, k))
        put_b((4 - d) % 4)

    def w_along_y():
        for d in STEPS:
            mail.arrived(s_wz[d], wz_in.at[d - 1], device(y, (z + 4 - d) % 4, core))
        here = pl.ds(pl.multiple_of(z * wq, 16), wq)
        total = wsum[here, :]
        for d in STEPS:
            total = total + wz_in[d - 1].astype(F32)
        wsum[here, :] = total
        wy_out[...] = total.astype(BF16)
        for d in STEPS:
            mail.start(s_wy[d], wy_out, wy_in.at[d - 1], device((y + d) % 4, z, core))

    def w_back():
        for d in STEPS:
            mail.arrived(s_wy[d], wy_in.at[d - 1], device((y + 4 - d) % 4, z, core))
        at = pl.ds(pl.multiple_of(z * wq, 16), wq)
        total = wsum[at, :]
        for d in STEPS:
            total = total + wy_in[d - 1].astype(F32)
        wfull[at, :] = total.astype(BF16)
        for d in STEPS:
            mail.start(s_wa[d], wfull.at[at], wfull.at[at], device(y, (z + d) % 4, core))

    w_along_y()
    relay(1)
    relay(3)
    w_back()
    relay(2)
    for q in range(1, 4):
        rechunk_four(q)
    height, breadth = target.shape[0], target.shape[1]
    top_rows, end_rows = pl.ds(0, 2), pl.ds(height - 2, 2)
    lead, trail = pl.ds(0, LEAD), pl.ds(breadth - LEAD, LEAD)
    borders = {
        (1, 0): (target.at[end_rows], t_rows.at[0]),
        (-1, 0): (target.at[top_rows], t_rows.at[1]),
        (0, 1): (target.at[:, trail], t_cols.at[0]),
        (0, -1): (target.at[:, lead], t_cols.at[1]),
        (1, 1): (target.at[end_rows, trail], t_ends.at[0]),
        (1, -1): (target.at[end_rows, lead], t_ends.at[1]),
        (-1, 1): (target.at[top_rows, trail], t_ends.at[2]),
        (-1, -1): (target.at[top_rows, lead], t_ends.at[3]),
    }
    s_border = mail.slots(NEXT)
    for to in NEXT:
        mail.start(s_border[to], *borders[to], tile_peer(*to))
    xp[...] = dot(tokens[...], proj[...]).reshape(xp.shape)

    sib_rows = pl.ds(pl.multiple_of(other * here_rows, 128), here_rows)
    for q in range(4):
        four = pl.ds(4 * q, 4)
        mail.arrived(s_n[q, 0], nrm.at[four, sib_rows], sibling)
        mail.arrived(s_n[q, 1], nrmt.at[four, :, sib_rows], sibling)
    keep = [pltpu.make_async_copy(nrmt, nrmt_hbm, local.at[0])]
    keep[0].start()

    def multiply(blocks, first=False):
        total = None
        for da, db in blocks:
            at = block(da, db)
            term = dot(nrm[at], gath[at])
            total = term if total is None else total + term
        pre[...] = total if first else pre[...] + total

    def take_b(da, d):
        mail.arrived(s_b[da, d], gath.at[block(da, -d)], peer(0, -d))

    multiply([(0, 0), (3, 0)], first=True)
    multiply([(1, 0), (2, 0)])
    for da in (0, 3, 1, 2):
        take_b(da, 1)
        take_b(da, 3)
        multiply([(da, 3), (da, 1)])
        take_b(da, 2)
        multiply([(da, 2)])

    a_all = gelu_tanh(pre[...]).astype(BF16)
    act[...] = a_all
    for d in STEPS:
        frm = (z + 4 - d) % 4
        at = pl.ds(pl.multiple_of(frm * wq, 16), wq)
        mail.arrived(s_wa[d], wfull.at[at], device(y, frm, core))
    n_out = fold.shape[1]
    fold[...] = jnp.where(grp == 0, wfull[:, :n_out], wfull[:, n_out:])

    n_rows, n_cols = xp.shape[0], xp.shape[1]
    for k in range(2):
        at = pl.ds(k * here_rows, here_rows)
        part[k] = dot(act[at, :], fold[...]).reshape(part.shape[1:])
    s_part = mail.slot()
    mail.start(s_part, part.at[other], part_in, sibling)
    own_cols = pl.ds(pl.multiple_of(tile * (n_cols // 4), 16), n_cols // 4)
    part[core, :, own_cols, :] = part[core, :, own_cols, :] + xp[:, own_cols, :]
    keep.append(pltpu.make_async_copy(act, act_hbm, local.at[1]))
    keep[1].start()
    mail.arrived(s_part, part_in, sibling)
    total = part[core] + part_in[...]

    edge = jnp.zeros((n_rows // 2, EDGE, 2 * n_out), F32)
    psrc[:, :EDGE, :] = edge
    psrc[:, EDGE + n_cols :, :] = edge
    psrc[:, EDGE : EDGE + n_cols, :] = jnp.concatenate(
        [total[: n_rows // 2], total[n_rows // 2 :]], axis=2
    )
    span = main_in.shape[2]

    def window(dt):
        return pl.ds(pl.multiple_of((tile + dt) % 4 * (n_cols // 4), 8), span)

    s_around = mail.slots(AROUND)
    for ds, dt in AROUND:
        if ds == 0:
            src, dst = psrc.at[:, window(dt)], main_in.at[dt]
        elif ds == -1:
            src, dst = psrc.at[pl.ds(0, 1), window(dt)], edge_in.at[1, dt]
        else:
            src, dst = psrc.at[pl.ds(n_rows // 2 - 1, 1), window(dt)], edge_in.at[0, dt]
        mail.start(s_around[ds, dt], src, dst, tile_peer(ds, dt))
    pre[...] = gelu_slope(pre[...])
    keep.append(pltpu.make_async_copy(pre, slope_hbm, local.at[2]))
    keep[2].start()

    total = psrc[:, window(0), :]
    for dt in range(1, 4):
        mail.arrived(s_around[0, dt], main_in.at[dt], tile_peer(0, -dt))
        total = total + main_in[dt]
    sums[1 : 1 + n_rows // 2] = total[:, :, :n_out]
    sums[1 + n_rows // 2 : 1 + n_rows] = total[:, :, n_out:]
    seq = lax.axis_index("seq")
    for i, ds in ((0, 1), (1, -1)):
        total = jnp.zeros(edge_in.shape[3:], F32)
        for dt in range(4):
            mail.arrived(s_around[ds, dt], edge_in.at[i, dt], tile_peer(-ds, -dt))
            total = total + edge_in[i, dt, 0]
        outside = (seq == 0) if i == 0 else (seq == 15)
        total = total[:, n_out:] if i == 0 else total[:, :n_out]
        sums[(n_rows + 1) * i] = jnp.where(outside, 0.0, total)

    for ds, dt in NEXT:
        mail.arrived(s_border[ds, dt], borders[ds, dt][1], tile_peer(-ds, -dt))
    for copy in keep:
        copy.wait()
    mail.finish()


def forward(tokens, shift, scale, proj, fc1, fc2, gps, target):
    rows, width = tokens.shape
    depth, hidden = fc1.shape
    half = hidden // 2
    n_out = proj.shape[1]
    n_blk = 16
    height, breadth, ch = target.shape
    token_rows, n_cols = 4 * rows // 512, 128
    span = n_cols // 4 + 2 * EDGE
    vmem, hbm = pl.BlockSpec(memory_space=VMEM), pl.BlockSpec(memory_space=pl.ANY)
    shape = jax.ShapeDtypeStruct
    return pl.pallas_call(
        forward_kernel,
        out_shape=(
            shape((2 * rows, half), F32),
            shape((2 * rows, half), BF16),
            shape((token_rows + 2, span, n_out), F32),
            shape((half, n_out), BF16),
            shape(gps.shape[1:], F32),
            shape((n_blk, 2 * depth, 2 * rows), BF16),
            shape((2, 2, breadth, ch), BF16),
            shape((2, height, LEAD, ch), BF16),
            shape((4, 2, LEAD, ch), BF16),
        ),
        in_specs=[vmem] * 7 + [hbm],
        out_specs=(hbm, hbm, vmem, vmem, vmem, hbm, hbm, hbm, hbm),
        scratch_shapes=[
            VMEM((rows, width), BF16),
            VMEM((n_blk, 2 * rows, 2 * depth), BF16),
            VMEM((n_blk, 2 * depth, 2 * rows), BF16),
            VMEM((n_blk, 2 * depth, half), BF16),
            VMEM(gps.shape[1:], F32),
            VMEM((hidden, 2 * n_out), F32),
            VMEM((half, 2 * n_out), F32),
            VMEM((half, 2 * n_out), F32),
            VMEM((half, 2 * n_out), BF16),
            VMEM((3, half // 4, 2 * n_out), BF16),
            VMEM((half // 4, 2 * n_out), BF16),
            VMEM((3, half // 4, 2 * n_out), BF16),
            VMEM((half, 2 * n_out), BF16),
            VMEM((token_rows, n_cols, n_out), F32),
            VMEM((2 * rows, half), F32),
            VMEM((2 * rows, half), BF16),
            VMEM((2, token_rows, n_cols, n_out), F32),
            VMEM((token_rows, n_cols, n_out), F32),
            VMEM((token_rows // 2, n_cols + 2 * EDGE, 2 * n_out), F32),
            VMEM((4, token_rows // 2, span, 2 * n_out), F32),
            VMEM((2, 4, 1, span, 2 * n_out), F32),
            pltpu.SemaphoreType.DMA((72,)),
            pltpu.SemaphoreType.DMA((72,)),
            pltpu.SemaphoreType.DMA((3,)),
        ],
        compiler_params=pltpu.CompilerParams(
            collective_id=1, has_side_effects=True, vmem_limit_bytes=58 * 2**20
        ),
    )(tokens, shift, scale, proj, fc1, fc2, gps, target)


def pixel_kernels(lift, conv_a):
    lifted = {
        (o, e): dot(lift, conv_a[3 * o + e])
        for o in range(3)
        for e in range(3)
    }

    def reach(pixel, cell):
        return [o for o in range(3) if (pixel + o - 1) // 2 == cell]

    out = {}
    for r in range(-1, 5):
        for c in range(-1, 5):
            parts = []
            for a in range(2):
                for b in range(2):
                    total = jnp.zeros_like(lifted[0, 0])
                    for o in reach(r, a):
                        for e in reach(c, b):
                            total = total + lifted[o, e]
                    parts.append(total)
            out[r, c] = jnp.concatenate(parts, axis=0)
    return out


def middle_kernel(
    sums, lift, conv_a, conv_b, conv_bt, target, t_rows, t_cols, t_ends,
    latent, lg,
    patch, kern, f_ref, a_ref, b_ref, acc, want, gf, send, recv,
):
    grp, seq, tile = lax.axis_index("grp"), lax.axis_index("seq"), lax.axis_index("tile")
    core = seq % 2

    def cores(k, dt):
        return (grp, seq - core + (core + k) % 2, (tile + dt) % 4)

    around = [(k, dt) for k in range(2) for dt in range(4) if (k, dt) != (0, 0)]
    announce([cores(k, dt) for k, dt in around])
    mail = Courier(send, recv)
    n_tok, span, width = sums.shape
    n_rows, here = n_tok - 2, span - 2 * EDGE
    pairs, ch = a_ref.shape[1], a_ref.shape[2] // 4

    kernels = pixel_kernels(lift[...], conv_a)
    for r in range(-1, 5):
        for c in range(-1, 5):
            kern[6 * (r + 1) + c + 1] = kernels[r, c].astype(BF16)
    height, breadth = target.shape[0], target.shape[1]
    body, lead = slice(LEAD, LEAD + breadth), slice(0, LEAD)
    trail = slice(LEAD + breadth, 2 * LEAD + breadth)
    mid = slice(2, 2 + height)

    def want_at(rows, at, value):
        value = value.astype(F32)
        want[rows, 0, at, :] = value[:, :, :128]
        want[rows, 1, at, :] = value[:, :, 128:]

    want_at(mid, body, target[...])
    want_at(slice(0, 2), body, t_rows[0])
    want_at(slice(2 + height, 4 + height), body, t_rows[1])
    for side, at in ((0, lead), (1, trail)):
        want_at(mid, at, t_cols[side])
        want_at(slice(0, 2), at, t_ends[side])
        want_at(slice(2 + height, 4 + height), at, t_ends[2 + side])

    rows = {r: sums[r] for r in range(n_tok)}
    for r in range(n_tok):
        patch[0, r + 1] = pltpu.roll(rows[r], 1, 0).astype(BF16)
        patch[1, r + 1] = rows[r].astype(BF16)
        patch[2, r + 1] = pltpu.roll(rows[r], span - 1, 0).astype(BF16)
    for k in range(3):
        patch[k, 0] = jnp.zeros((span, width), BF16)
        patch[k, n_tok + 1] = jnp.zeros((span, width), BF16)

    def near(phase):
        return [(d, phase - 4 * d) for d in (-1, 0, 1) if -1 <= phase - 4 * d <= 4]

    for al in range(4):
        for ph in range(4):
            value = None
            for dr, r in near(al):
                for dc, c in near(ph):
                    lhs = patch[1 + dc, 1 + dr : 1 + dr + n_tok].reshape(n_tok * span, width)
                    term = dot(lhs, kern[6 * (r + 1) + c + 1])
                    value = term if value is None else value + term
            value = value.reshape(n_tok, span, ch)
            for tr in range(n_tok):
                at = pl.ds(ph // 2, span, stride=2)
                f_ref[4 * tr + al, ph % 2, 0, at, :] = value[tr, :, :128]
                f_ref[4 * tr + al, ph % 2, 1, at, :] = value[tr, :, 128:]

    def inside(row, b):
        r = seq * height + row
        c = 2 * (tile * breadth // 2 + lax.broadcasted_iota(jnp.int32, (pairs, 1), 0) - EDGE) + b
        return (r >= 0) & (r < 16 * height) & (c >= 0) & (c < 4 * breadth)

    def both(ref, at, rows):
        return jnp.concatenate([ref[*at, 0, rows, :], ref[*at, 1, rows, :]], axis=1)

    def spread(ref, at, v0, v1):
        ref[at, :, 0:ch] = pltpu.roll(v1, 1, 0).astype(BF16)
        ref[at, :, ch : 2 * ch] = v0.astype(BF16)
        ref[at, :, 2 * ch : 3 * ch] = v1.astype(BF16)
        ref[at, :, 3 * ch :] = pltpu.roll(v0, pairs - 1, 0).astype(BF16)

    @pl.loop(0, height + 6)
    def _(i):
        smooth = []
        for b in range(2):
            f = both(f_ref, (i + 1, b), slice(EDGE, EDGE + pairs))
            sigma = jax.nn.sigmoid(f)
            smooth.append(jnp.where(inside(i - 3, b), f * sigma, 0.0))
            slope = sigma * (1.0 + f * (1.0 - sigma))
            f_ref[i + 1, b, 0, EDGE : EDGE + pairs, :] = slope[:, :128]
            f_ref[i + 1, b, 1, EDGE : EDGE + pairs, :] = slope[:, 128:]
        spread(a_ref, i, *smooth)

    def conv(src, weights, out_rows, chunk):
        @pl.loop(0, out_rows // chunk)
        def _(i):
            for b in range(2):
                value = None
                for o in range(3):
                    lhs = src[pl.ds(i * chunk + o, chunk), :, b * ch : (b + 3) * ch]
                    term = dot(lhs.reshape(chunk * pairs, 3 * ch), weights[o])
                    value = term if value is None else value + term
                acc[b, pl.ds(i * chunk, chunk)] = value.reshape(chunk, pairs, ch)

    conv(a_ref, conv_b, height + 4, (height + 4) // 2)

    @pl.loop(0, height + 4)
    def _(i):
        grad = []
        for b in range(2):
            diff = acc[b, i] - both(want, (i,), pl.ds(b, pairs, stride=2))
            grad.append(jnp.where(inside(i - 2, b), diff, 0.0))
        spread(b_ref, i, *grad)

    conv(b_ref, conv_bt, height + 2, (height + 2) // 2)

    @pl.loop(0, height + 2)
    def _(i):
        for b in range(2):
            value = acc[b, i] * both(f_ref, (i + 3, b), slice(EDGE, EDGE + pairs))
            value = jnp.where(inside(i - 1, b), value, 0.0)
            gf[i, b, 0], gf[i, b, 1] = value[:, :128], value[:, 128:]

    grad = None
    for r in range(-1, 5):
        for c in range(-1, 5):
            at = pl.ds(EDGE + c // 2, here, stride=2)
            lhs = jnp.concatenate(
                [both(gf, (4 * tr + r + 1, c % 2), at).astype(BF16) for tr in range(n_rows)],
                axis=0,
            )
            term = dot(lhs, kern[6 * (r + 1) + c + 1], NT)
            grad = term if grad is None else grad + term
    grad = grad.reshape(n_rows, here, width)
    latent[...] = grad
    def part_of(k, dt):
        cols = pl.ds(pl.multiple_of((tile + dt) % 4 * here, 16), here)
        return lg.at[pl.ds((core + k) % 2 * n_rows, n_rows), cols]

    cols = pl.ds(pl.multiple_of(tile * here, 16), here)
    lg[pl.ds(core * n_rows, n_rows), cols, :] = grad.astype(BF16)
    await_peers(around)
    s_back = mail.slots(around)
    for k, dt in around:
        mail.start(s_back[k, dt], part_of(0, 0), part_of(0, 0), cores(k, dt))
    for k, dt in around:
        mail.arrived(s_back[k, dt], part_of(k, -dt), cores(k, -dt))
    mail.finish()


def middle(sums, lift, conv_a, conv_b, conv_bt, target, t_rows, t_cols, t_ends):
    n_tok, span, width = sums.shape
    n_rows, here = n_tok - 2, span - 2 * EDGE
    height, breadth, ch = target.shape
    pairs = breadth // 2 + 2 * EDGE
    vmem = pl.BlockSpec(memory_space=VMEM)
    shape = jax.ShapeDtypeStruct
    return pl.pallas_call(
        middle_kernel,
        out_shape=(
            shape((n_rows, here, width), F32),
            shape((2 * n_rows, 4 * here, width), BF16),
        ),
        in_specs=[vmem] * 9,
        out_specs=(vmem,) * 2,
        scratch_shapes=[
            VMEM((3, n_rows + 4, span, width), BF16),
            VMEM((36, width, ch), BF16),
            VMEM((height + 8, 2, 2, 2 * span, ch // 2), F32),
            VMEM((height + 6, pairs, 4 * ch), BF16),
            VMEM((height + 4, pairs, 4 * ch), BF16),
            VMEM((2, height + 4, pairs, ch), F32),
            VMEM((height + 4, 2, breadth + 2 * LEAD, ch // 2), F32),
            VMEM((height + 2, 2, 2, pairs, ch // 2), F32),
            pltpu.SemaphoreType.DMA((40,)),
            pltpu.SemaphoreType.DMA((40,)),
        ],
        compiler_params=pltpu.CompilerParams(
            collective_id=3, has_side_effects=True, vmem_limit_bytes=58 * 2**20
        ),
    )(sums, lift, conv_a, conv_b, conv_bt, target, t_rows, t_cols, t_ends)
def backward_kernel(
    nrmt_hbm, slope_hbm, act_hbm, fold, lg, gboth, out, two,
    nrmt, slope, act, gpre, st, sz_in, sy_out, sy_in, sfull, b_out, b_in, a_out, a_in, fin, fin_in,
    send, recv, local,
):
    y, z, core, device = place()
    a, b, turn = oriented(y, z, core)
    grp = lax.axis_index("grp")
    other = 1 - core
    sibling = device(y, z, other)
    peers = (
        [sibling]
        + [device((y + d) % 4, z, core) for d in STEPS]
        + [device(y, (z + d) % 4, core) for d in STEPS]
    )
    announce(peers)
    loads = [
        pltpu.make_async_copy(src, dst, local.at[i])
        for i, (src, dst) in enumerate(
            ((act_hbm, act), (slope_hbm, slope), (nrmt_hbm, nrmt))
        )
    ]
    for load in loads:
        load.start()
    mail = Courier(send, recv)
    half = gpre.shape[1]
    rows = nrmt.shape[1] // 2

    def peer(da, db):
        return device(*turn((a + da) % 4, (b + db) % 4), core)

    def block(da, db):
        return block_of(*turn((a + da) % 4, (b + db) % 4))

    def term(da, db):
        return dot(nrmt[block(da, db)], gpre[...])

    s_b = mail.slots((da, d) for da in range(4) for d in STEPS)
    s_a = mail.slots(STEPS)

    def send_b(da):
        for d in (2, 1, 3):
            b_out[da, d - 1] = term(da, d).astype(BF16)
            mail.start(s_b[da, d], b_out.at[da, d - 1], b_in.at[da, d - 1], peer(0, d))

    def sum_b(da):
        total = term(da, 0)
        for d in STEPS:
            mail.arrived(s_b[da, d], b_in.at[da, d - 1], peer(0, -d))
            total = total + b_in[da, d - 1].astype(F32)
        return total

    def send_a(d):
        a_out[d - 1] = sum_b(d).astype(BF16)
        mail.start(s_a[d], a_out.at[d - 1], a_in.at[d - 1], peer(d, 0))

    loads[0].wait()
    st[...] = dot(lg[...], act[...], TN)
    sq = st.shape[0] // 4
    s_sz, s_sy, s_sa = mail.slots(STEPS), mail.slots(STEPS), mail.slots(STEPS)
    await_peers(peers)
    for d in STEPS:
        to = (z + d) % 4
        src = st.at[pl.ds(pl.multiple_of(to * sq, 8), sq)]
        mail.start(s_sz[d], src, sz_in.at[d - 1], device(y, to, core))

    loads[1].wait()
    gpre[...] = (dot(lg[...], fold[...], NT) * slope[...]).astype(BF16)
    loads[2].wait()
    send_b(2)

    for d in STEPS:
        mail.arrived(s_sz[d], sz_in.at[d - 1], device(y, (z + 4 - d) % 4, core))
    s_at = pl.ds(pl.multiple_of(z * sq, 8), sq)
    sy_out[...] = st[s_at, :] + sz_in[0] + sz_in[1] + sz_in[2]
    for d in STEPS:
        mail.start(s_sy[d], sy_out, sy_in.at[d - 1], device((y + d) % 4, z, core))

    send_b(1)
    for d in STEPS:
        mail.arrived(s_sy[d], sy_in.at[d - 1], device((y + 4 - d) % 4, z, core))
    sfull[core, grp, s_at] = sy_out[...] + sy_in[1]
    sfull[core, 1 - grp, s_at] = sy_in[0] + sy_in[2]
    for d in STEPS:
        ref = sfull.at[core, :, s_at]
        mail.start(s_sa[d], ref, ref, device(y, (z + d) % 4, core))
    send_b(3)
    send_b(0)

    send_a(2)
    for d in STEPS:
        frm = (z + 4 - d) % 4
        at = pl.ds(pl.multiple_of(frm * sq, 8), sq)
        mail.arrived(s_sa[d], sfull.at[core, :, at], device(y, frm, core))
    s_ss = mail.slot()
    mail.start(s_ss, sfull.at[core], sfull.at[core], sibling)
    send_a(1)
    send_a(3)

    mail.arrived(s_ss, sfull.at[other], sibling)
    g_high, g_low = split(gboth[...])
    for h in range(2):
        s_high, s_low = split(sfull[h].reshape(-1, half).T)
        value = dot(s_high, g_high, NT) + dot(s_high, g_low, NT) + dot(s_low, g_high, NT)
        two[h * half : (h + 1) * half, :] = value[:, : two.shape[1]]

    total = sum_b(0)
    for d in STEPS:
        mail.arrived(s_a[d], a_in.at[d - 1], peer(-d, 0))
        total = total + a_in[d - 1].astype(F32)
    fin[...] = total
    s_fin = mail.slot()
    theirs = pl.ds(pl.multiple_of(other * rows, 16), rows)
    mail.start(s_fin, fin.at[theirs], fin_in, sibling)
    here = out.shape[0]
    mine = fin[pl.ds(pl.multiple_of(core * rows, 16), rows), :]
    out[:, pl.ds(pl.multiple_of(core * half, 128), half)] = mine[:here]
    mail.arrived(s_fin, fin_in, sibling)
    out[:, pl.ds(pl.multiple_of(other * half, 128), half)] = fin_in[:here, :]
    mail.finish()


def backward(nrmt, slope, act, fold, lg, gboth, here):
    n_blk, depth, rows = nrmt.shape
    half = slope.shape[1]
    width = lg.shape[1]
    vmem, hbm = pl.BlockSpec(memory_space=VMEM), pl.BlockSpec(memory_space=pl.ANY)
    shape = jax.ShapeDtypeStruct
    return pl.pallas_call(
        backward_kernel,
        out_shape=(shape((here, 2 * half), F32), shape((2 * half, here), F32)),
        in_specs=[hbm] * 3 + [vmem] * 3,
        out_specs=(vmem,) * 2,
        scratch_shapes=[
            VMEM(nrmt.shape, BF16),
            VMEM(slope.shape, F32),
            VMEM(act.shape, BF16),
            VMEM((rows, half), BF16),
            VMEM((width, half), F32),
            VMEM((3, width // 4, half), F32),
            VMEM((width // 4, half), F32),
            VMEM((3, width // 4, half), F32),
            VMEM((2, 2, width, half), F32),
            VMEM((4, 3, depth, half), BF16),
            VMEM((4, 3, depth, half), BF16),
            VMEM((3, depth, half), BF16),
            VMEM((3, depth, half), BF16),
            VMEM((depth, half), F32),
            VMEM((depth // 2, half), F32),
            pltpu.SemaphoreType.DMA((32,)),
            pltpu.SemaphoreType.DMA((32,)),
            pltpu.SemaphoreType.DMA((3,)),
        ],
        compiler_params=pltpu.CompilerParams(
            collective_id=2, has_side_effects=True, vmem_limit_bytes=58 * 2**20
        ),
    )(nrmt, slope, act, fold, lg, gboth)


def shards(tokens, shift, scale, gate, fc1, fc2, proj, lift, conv_a, conv_b, target):
    width = tokens.shape[3]
    n_seq = lax.axis_size("seq")
    seq, grp = lax.axis_index("seq"), lax.axis_index("grp")
    patch_width = proj.shape[1]

    cols_here = fc2.shape[1]
    gps = []
    for at in (grp, 1 - grp):
        col_at = (at * n_seq + seq) * cols_here
        gate_cols = lax.dynamic_slice_in_dim(gate[0], col_at, cols_here, 0)
        proj_cols = lax.dynamic_slice_in_dim(proj, col_at, cols_here, 0)
        here = gate_cols[:, None] * proj_cols.astype(F32)
        zero = jnp.zeros_like(here)
        pair = [jnp.where(grp == i, here, zero) for i in range(2)]
        gps.append(jnp.concatenate(pair, axis=1))
    gps = jnp.pad(jnp.stack(gps), ((0, 0), (0, 4), (0, 0)))

    slope, act, sums, fold, gboth, nrmt, *borders = forward(
        tokens[0].reshape(-1, width),
        shift,
        scale,
        proj,
        jnp.pad(fc1, ((0, 4), (0, 0))),
        fc2,
        gps,
        target[0],
    )
    ch = conv_a.shape[2]
    conv_bt = jnp.swapaxes(conv_b[::-1, ::-1], 2, 3).reshape(3, 3 * ch, ch)
    latent_mine, latent_rows = middle(
        sums,
        lift,
        conv_a.reshape(9, ch, ch),
        conv_b.reshape(3, 3 * ch, ch),
        conv_bt,
        target[0],
        *borders,
    )
    latent_rows = latent_rows.reshape(-1, patch_width)
    grad_one, grad_two = backward(nrmt, slope, act, fold, latent_rows, gboth, cols_here)
    return (grad_one, grad_two, latent_mine[None])


def solution(mesh):
    in_specs = (
        P("grp", "seq", None, None),
        P("grp", None),
        P("grp", None),
        P("grp", None),
        P(("grp", "seq"), "tile"),
        P("tile", ("grp", "seq")),
        P(),
        P(),
        P(),
        P(),
        P("grp", "seq", "tile", None),
    )
    out_specs = (
        P(("grp", "seq"), "tile"),
        P("tile", ("grp", "seq")),
        P("grp", "seq", "tile", None),
    )
    return jax.shard_map(shards, mesh=mesh, in_specs=in_specs, out_specs=out_specs, check_vma=False)
```

time: 497 us -> 133 us (0.27); the launches traced: 487 us -> 132 us
  waiting for transfers between devices: 301 us -> 0 us
  Pallas kernels: 0 us -> 122 us
  matrix products: 56.3 us -> 0 us
  starting transfers between devices: 40.4 us -> 0 us
  local copies, waits for them, and re-layouts: 38.3 us -> 8.87 us
  other arithmetic: 26.3 us -> 0.86 us
  between operations: 15.3 us -> 0.74 us
  blocking collectives: 9.34 us -> 0 us
    unnamed x5 -> x0, waiting for transfers between devices: 135 us -> none
    pallas_call x0 -> x3, Pallas kernels: none -> 122 us  [the longest x1 61.1 us: forward(): pl.pallas_call(forward_kernel, out_shape=(shape((2 * rows, half), F32), s...]
    all_gather x2 -> x0, waiting for transfers between devices: 104 us -> none  [the longest x1 55.8 us: shards(): lax.all_gather(fc1, ('grp', 'seq'), axis=0, tiled=True)]
    dot_general x46 -> x0, matrix products: 56.3 us -> none  [the longest x36 19.9 us: conv_tile(): jnp.dot(window, kernel[row_off, col_off], preferred_element_type=jnp.floa...]
    ppermute x16 -> x0, starting transfers between devices: 40.3 us -> none  [the longest x8 27.2 us: padded_2(): before = lax.ppermute(last, axis, up)]
    psum x1 -> x0, waiting for transfers between devices: 35.7 us -> none  [shards(): lax.psum(partial_value.astype(jnp.bfloat16), 'tile').astype(jnp.float32)]
    ppermute x16 -> x0, waiting for transfers between devices: 27 us -> none  [the longest x8 27 us: padded_2(): after = lax.ppermute(leading, axis, down)]
    unnamed x34 -> x17, local copies, waits for them, and re-layouts: 26.2 us -> 5.74 us
  transfers between devices with their start and end apart: 20 -> 0, of which waited for: 12 -> 0; matrix products, arithmetic and copies ran while one was open for 8% -> 0% of each run, Pallas kernels for 0% -> 0%
where the time goes in v2:
time: 133 us; the launch traced here: 132 us
  Pallas kernels  122 us (92%)
  local copies, waits for them, and re-layouts  8.87 us (7%)
    pallas_call x1, Pallas kernels, forward(): pl.pallas_call(forward_kernel, out_shape=(shape((2 * rows, half), F32), s...  61.1 us
    pallas_call x1, Pallas kernels, backward(): pl.pallas_call(backward_kernel, out_shape=(shape((here, 2 * half), F32),...  36.1 us
    pallas_call x1, Pallas kernels, middle(): pl.pallas_call(middle_kernel, out_shape=(shape((n_rows, here, width), F32...  24.6 us
    unnamed x17, local copies, waits for them, and re-layouts  5.74 us

profile of v2, /device:TPU:1, one launch (start us, length us, event | category | flops | bytes accessed | tf_op | source)
XLA Modules:
  0.0 132.4 jit_solution(15495595689419526347)
XLA Ops:
  0.6 0.0 copy-start.4
  0.6 0.0 copy-start.3
  0.7 0.8 fusion.4
  1.5 1.3 copy.16.proj
  2.8 0.0 copy-start.1
  2.8 0.1 fusion.3
  2.9 0.1 maximum_bitcast_fusion
  3.0 0.7 select_maximum_fusion.gps
  3.7 0.0 copy-done.4
  3.7 0.9 copy.17.fc2
  4.6 0.0 copy-done.3
  4.6 0.7 pad.8.fc1
  5.3 0.0 copy-done.1
  5.3 0.0 copy-start
  5.3 61.1 %shard_map.130 = (f32[1024,640]{1,0:T(8,128)}, bf16[1024,640]{1,0:T(8,128)(2,1)}, f32[6,48,64]{2,1,0:T(8,128)}, bf16[640,64]{1,0:T(8,128)(2,1)}, f32[80,128]{1,0...) custom-call(bf16[512,2432]{1,0:T(8,128)(2,1)} %bitcast.21, ...), custom_call_target="tpu_custom_call" | custom-call | tf_op jit(solution)/shard_map/pallas_call | solution.py:394
  66.4 0.0 copy-done
  66.4 0.1 reverse_bitcast_fusion
  66.5 1.5 %copy.18 = bf16[3,3,256,256]{3,2,1,0:T(8,128)(2,1)} copy(bf16[3,3,256,256]{2,3,1,0:T(8,128)(2,1)S(1)} %reverse_bitcast_fusion) | data formatting | bytes 2359296 | tf_op jit(solution)/shard_map/transpose | solution.py:834
  68.0 24.6 %shard_map.131 = (f32[4,32,64]{2,1,0:T(8,128)}, bf16[8,128,64]{2,1,0:T(8,128)(2,1)}) custom-call(f32[6,48,64]{2,1,0:T(8,128)} %get-tuple-element.20.sums, bf16[16,256]{1,0:T(8,128)(2,1)} %lift.1, bf16[9,256,256]{2,1,0:T(8,128)(2,1)} %bitcast.22, bf16[3,768,256]{2,1,0:T(8,128)(2,1)} %bitcast.17, bf16[3,768,256]{2,1,0:T(8,128)(2,1)} %bitcast.18, ...), custom_call_target="tpu_custom_call" | custom-call | tf_op jit(solution)/shard_map/pallas_call | solution.py:622
  92.7 36.1 %shard_map.132 = (f32[76,1280]{1,0:T(8,128)}, f32[1280,76]{1,0:T(8,128)}) custom-call(bf16[16,160,1024]{2,1,0:T(8,128)(2,1)} %get-tuple-element.16.nrmt_hbm, f32[1024,640]{1,0:T(8,128)} %get-tuple-element.17.slope_hbm, bf16[1024,640]{1,0:T(8,128)(2,1)} %get-tuple-element.18.act_hbm, bf16[640,64]{1,0:T(8,128)(2,1)} %get-tuple-element.19.fold, ...), custom_call_target="tpu_custom_call" | custom-call | tf_op jit(solution)/shard_map/pallas_call | solution.py:774
  128.8 0.0 copy-start.2
  128.8 0.0 copy-start.5
  128.8 2.1 %copy.19 = f32[1280,76]{0,1:T(8,128)} copy(f32[1280,76]{1,0:T(8,128)} %get-tuple-element.30) | data formatting | bytes 778240
  131.0 0.0 copy-done.2
  131.0 0.8 copy.22
  131.7 0.0 copy-done.5
  131.7 0.6 copy.23
Async XLA Ops:
  0.6 3.0 %copy-start.4 = (bf16[1280,76]{0,1:T(8,128)(2,1)S(1)}, bf16[1280,76]{0,1:T(8,128)(2,1)}, u32[]{:S(2)}) copy-start(bf16[1280,76]{0,1:T(8,128)(2,1)} %param.16) | copy-start | bytes 583684
  0.6 3.9 %copy-start.3 = (bf16[76,1280]{1,0:T(8,128)(2,1)S(1)}, bf16[76,1280]{1,0:T(8,128)(2,1)}, u32[]{:S(2)}) copy-start(bf16[76,1280]{1,0:T(8,128)(2,1)} %param.15) | copy-start | bytes 583684
  2.8 2.5 %copy-start.1 = (bf16[2432,64]{1,0:T(8,128)(2,1)}, bf16[2432,64]{1,0:T(8,128)(2,1)S(1)}, u32[]{:S(2)}) copy-start(bf16[2432,64]{1,0:T(8,128)(2,1)S(1)} %copy.16.proj) | copy-start | bytes 933892
  5.3 61.1 %copy-start = (bf16[3,3,256,256]{3,2,1,0:T(8,128)(2,1)S(1)}, bf16[3,3,256,256]{3,2,1,0:T(8,128)(2,1)}, u32[]{:S(2)}) copy-start(bf16[3,3,256,256]{3,2,1,0:T(8,128)(2,1)} %param.20) | copy-start | bytes 3538948
  128.8 2.2 %copy-start.2 = (f32[76,1280]{1,0:T(8,128)S(1)}, f32[76,1280]{1,0:T(8,128)}, u32[]{:S(2)}) copy-start(f32[76,1280]{1,0:T(8,128)} %get-tuple-element.45) | copy-start | bytes 1167364
  128.8 2.9 %copy-start.5 = (f32[4,32,64]{2,1,0:T(8,128)S(1)}, f32[4,32,64]{2,1,0:T(8,128)}, u32[]{:S(2)}) copy-start(f32[4,32,64]{2,1,0:T(8,128)} %get-tuple-element.28) | copy-start | bytes 98308

commit v3 on v2

--- a/solution.py
+++ b/solution.py
@@ -118,10 +118,36 @@
             copy.wait_send()
 
 
+def pixel_kernels(lift, conv_a):
+    lifted = {
+        (o, e): dot(lift, conv_a[3 * o + e])
+        for o in range(3)
+        for e in range(3)
+    }
+
+    def reach(pixel, cell):
+        return [o for o in range(3) if (pixel + o - 1) // 2 == cell]
+
+    out = {}
+    for r in range(-1, 5):
+        for c in range(-1, 5):
+            parts = []
+            for a in range(2):
+                for b in range(2):
+                    total = jnp.zeros_like(lifted[0, 0])
+                    for o in reach(r, a):
+                        for e in reach(c, b):
+                            total = total + lifted[o, e]
+                    parts.append(total)
+            out[r, c] = jnp.concatenate(parts, axis=0)
+    return out
+
+
 def forward_kernel(
-    tokens, shift, scale, proj, fc1, fc2, gps, target,
-    slope_hbm, act_hbm, sums, fold, gboth, nrmt_hbm, t_rows, t_cols, t_ends,
-    normed, nrm, nrmt, gath, gin, wpart, wsib, wsum, wz_out, wz_in, wy_out, wy_in, wfull, xp,
+    tokens_hbm, shift, scale, gate, projt, fc1_own, fc2t, lift, conv_a_hbm, conv_b_hbm, target,
+    slope_hbm, act_hbm, sums, fold, gboth, nrmt_hbm, kern_hbm, conv_bt_hbm,
+    t_rows, t_cols, t_ends,
+    fc1, gps, tokens, conv_a, conv_b, kern, conv_bt, normed, nrm, nrmt, gath, gin, wpart, wsib, wsum, wz_out, wz_in, wy_out, wy_in, wfull, xp,
     pre, act, part, part_in, psrc, main_in, edge_in, send, recv, local,
 ):
     y, z, core, device = place()
@@ -129,15 +155,48 @@
     grp, tile = lax.axis_index("grp"), lax.axis_index("tile")
     other = 1 - core
     sibling = device(y, z, other)
-    greet(
+    peers = (
         [sibling]
         + [device((y + d) % 4, z, k) for d in STEPS for k in range(2)]
         + [device(y, (z + d) % 4, k) for d in STEPS for k in range(2)]
         + [tile_peer(ds, dt) for ds, dt in AROUND]
     )
+    announce(peers)
+    loads = [
+        pltpu.make_async_copy(src, dst, local.at[i])
+        for i, (src, dst) in enumerate(
+            ((tokens_hbm, tokens), (conv_a_hbm, conv_a), (conv_b_hbm, conv_b))
+        )
+    ]
+    for load in loads:
+        load.start()
     mail = Courier(send, recv)
     rows, half = gath.shape[1] // 2, gath.shape[2]
     here_rows, width = tokens.shape
+    cols = fc2t.shape[0]
+    last = cols // 16 * 16
+    fc1[:last] = fc1_own[:last]
+    tail = jnp.concatenate(
+        [fc1_own[last:].astype(F32), jnp.zeros((rows - cols, 2 * half), F32)], axis=0
+    )
+    fc1[last:] = tail.astype(BF16)
+
+    n_out = projt.shape[0]
+    seq = lax.axis_index("seq")
+    for i, g in enumerate((grp, 1 - grp)):
+        start = (g * 16 + seq) * cols
+        first = jnp.minimum(start // 128 * 128, width - 256)
+        at = pl.ds(pl.multiple_of(first, 128), 256)
+        high, low = split(gate[:, at] * projt[:, at].astype(F32))
+        r = lax.broadcasted_iota(jnp.int32, (rows, 256), 0)
+        k = lax.broadcasted_iota(jnp.int32, (rows, 256), 1)
+        pick = jnp.where((k == r + (start - first)) & (r < cols), 1.0, 0.0).astype(BF16)
+        value = dot(pick, high, NT) + dot(pick, low, NT)
+        zero = jnp.zeros_like(value)
+        gps[i] = jnp.concatenate(
+            [jnp.where(grp == 0, value, zero), jnp.where(grp == 1, value, zero)], axis=1
+        )
+    await_peers(peers)
 
     def peer(da, db):
         return device(*turn((a + da) % 4, (b + db) % 4), core)
@@ -162,26 +221,29 @@
             mail.start(s_a[h, d], src, gath.at[own, mine], to, r_a[d] + core)
     gath[own, mine, :] = fc1[:, pl.ds(pl.multiple_of(core * half, 128), half)]
 
+    loads[0].wait()
+
     @pl.loop(0, here_rows // 64)
     def _(i):
-        at = pl.ds(pl.multiple_of(i * 64, 64), 64)
-        x = tokens[at, :].astype(F32)
+        x = tokens[pl.ds(pl.multiple_of(i * 64, 64), 64), :].astype(F32)
         center = x - jnp.mean(x, axis=1, keepdims=True)
         spread = jnp.mean(center * center, axis=1, keepdims=True)
         value = center * lax.rsqrt(spread + 1e-06) * (1.0 + scale[...]) + shift[...]
+        at = pl.ds(pl.multiple_of(core * here_rows + i * 64, 64), 64)
         normed[at, :] = value.astype(BF16)
+
+    blk_rows = pl.ds(pl.multiple_of(core * here_rows, 128), here_rows)
+    s_n = mail.slot()
+    mail.start(s_n, normed.at[blk_rows], normed.at[blk_rows], sibling)
 
     mail.arrived(s_gate, gin, partner)
     both = gps[0] + gin[...]
     gboth[...] = both
-    high, low = split(both[: fc2.shape[1]])
-    wpart[...] = dot(fc2[...], high) + dot(fc2[...], low)
+    high, low = split(both[:cols])
+    wpart[...] = dot(fc2t[...], high, TN) + dot(fc2t[...], low, TN)
     wq = half // 4
     s_w = mail.slot()
     mail.start(s_w, wpart.at[pl.ds(pl.multiple_of(other * half, 16), half)], wsib, sibling)
-
-    blk_rows = pl.ds(pl.multiple_of(core * here_rows, 128), here_rows)
-    cols = fc2.shape[1]
 
     def rechunk(i):
         first = 2 * cols * i // 128 * 128
@@ -193,19 +255,8 @@
         high_part = (k == r + (off + cols - rows)) & (r >= rows) & (r < rows + cols)
         pick = jnp.where(low_part | high_part, 1.0, 0.0).astype(BF16)
         value = normed[:, first : first + span]
-        nrm[i, blk_rows, :] = dot(value, pick, NT).astype(BF16)
-        nrmt[i, :, blk_rows] = dot(pick, value, NT).astype(BF16)
-
-    s_n = mail.slots((q, k) for q in range(4) for k in range(2))
-
-    def rechunk_four(q):
-        for i in range(4 * q, 4 * q + 4):
-            rechunk(i)
-        four = pl.ds(4 * q, 4)
-        ref = nrm.at[four, blk_rows]
-        mail.start(s_n[q, 0], ref, ref, sibling)
-        ref = nrmt.at[four, :, blk_rows]
-        mail.start(s_n[q, 1], ref, ref, sibling)
+        nrm[i] = dot(value, pick, NT).astype(BF16)
+        nrmt[i] = dot(pick, value, NT).astype(BF16)
 
     mail.arrived(s_w, wsib, sibling)
     wsum[...] = wpart[pl.ds(pl.multiple_of(core * half, 16), half), :] + wsib[...]
@@ -225,7 +276,31 @@
 
     mail.arrived(s_own, gath.at[own, theirs], sibling)
     put_b(0)
-    rechunk_four(0)
+
+    keep = [
+        pltpu.make_async_copy(src, dst, local.at[3 + i])
+        for i, (src, dst) in enumerate(
+            (
+                (nrmt, nrmt_hbm),
+                (act, act_hbm),
+                (pre, slope_hbm),
+                (kern, kern_hbm),
+                (conv_bt, conv_bt_hbm),
+            )
+        )
+    ]
+    loads[1].wait()
+    kernels = pixel_kernels(lift[...], conv_a)
+    for i, value in enumerate(kernels.values()):
+        kern[i] = value.astype(BF16)
+    keep[3].start()
+    loads[2].wait()
+    ch = conv_b.shape[2]
+    for o in range(3):
+        for e in range(3):
+            conv_bt[o, e * ch : (e + 1) * ch, :] = conv_b[8 - 3 * o - e].T
+    keep[4].start()
+    xp[...] = dot(tokens[...], projt[...], NT).reshape(xp.shape)
 
     def relay(d):
         at = block(-d, 0)
@@ -263,8 +338,10 @@
     relay(3)
     w_back()
     relay(2)
-    for q in range(1, 4):
-        rechunk_four(q)
+    mail.arrived(s_n, normed.at[pl.ds(pl.multiple_of(other * here_rows, 128), here_rows)], sibling)
+    for i in range(gath.shape[0]):
+        rechunk(i)
+    keep[0].start()
     height, breadth = target.shape[0], target.shape[1]
     top_rows, end_rows = pl.ds(0, 2), pl.ds(height - 2, 2)
     lead, trail = pl.ds(0, LEAD), pl.ds(breadth - LEAD, LEAD)
@@ -281,15 +358,6 @@
     s_border = mail.slots(NEXT)
     for to in NEXT:
         mail.start(s_border[to], *borders[to], tile_peer(*to))
-    xp[...] = dot(tokens[...], proj[...]).reshape(xp.shape)
-
-    sib_rows = pl.ds(pl.multiple_of(other * here_rows, 128), here_rows)
-    for q in range(4):
-        four = pl.ds(4 * q, 4)
-        mail.arrived(s_n[q, 0], nrm.at[four, sib_rows], sibling)
-        mail.arrived(s_n[q, 1], nrmt.at[four, :, sib_rows], sibling)
-    keep = [pltpu.make_async_copy(nrmt, nrmt_hbm, local.at[0])]
-    keep[0].start()
 
     def multiply(blocks, first=False):
         total = None
@@ -311,24 +379,23 @@
         take_b(da, 2)
         multiply([(da, 2)])
 
-    a_all = gelu_tanh(pre[...]).astype(BF16)
-    act[...] = a_all
     for d in STEPS:
         frm = (z + 4 - d) % 4
         at = pl.ds(pl.multiple_of(frm * wq, 16), wq)
         mail.arrived(s_wa[d], wfull.at[at], device(y, frm, core))
-    n_out = fold.shape[1]
     fold[...] = jnp.where(grp == 0, wfull[:, :n_out], wfull[:, n_out:])
 
     n_rows, n_cols = xp.shape[0], xp.shape[1]
-    for k in range(2):
-        at = pl.ds(k * here_rows, here_rows)
-        part[k] = dot(act[at, :], fold[...]).reshape(part.shape[1:])
     s_part = mail.slot()
-    mail.start(s_part, part.at[other], part_in, sibling)
+    for k in (other, core):
+        at = pl.ds(pl.multiple_of(k * here_rows, 128), here_rows)
+        value = gelu_tanh(pre[at, :]).astype(BF16)
+        act[at, :] = value
+        part[k] = dot(value, fold[...]).reshape(part.shape[1:])
+        if k is other:
+            mail.start(s_part, part.at[other], part_in, sibling)
     own_cols = pl.ds(pl.multiple_of(tile * (n_cols // 4), 16), n_cols // 4)
     part[core, :, own_cols, :] = part[core, :, own_cols, :] + xp[:, own_cols, :]
-    keep.append(pltpu.make_async_copy(act, act_hbm, local.at[1]))
     keep[1].start()
     mail.arrived(s_part, part_in, sibling)
     total = part[core] + part_in[...]
@@ -354,7 +421,6 @@
             src, dst = psrc.at[pl.ds(n_rows // 2 - 1, 1), window(dt)], edge_in.at[0, dt]
         mail.start(s_around[ds, dt], src, dst, tile_peer(ds, dt))
     pre[...] = gelu_slope(pre[...])
-    keep.append(pltpu.make_async_copy(pre, slope_hbm, local.at[2]))
     keep[2].start()
 
     total = psrc[:, window(0), :]
@@ -363,7 +429,6 @@
         total = total + main_in[dt]
     sums[1 : 1 + n_rows // 2] = total[:, :, :n_out]
     sums[1 + n_rows // 2 : 1 + n_rows] = total[:, :, n_out:]
-    seq = lax.axis_index("seq")
     for i, ds in ((0, 1), (1, -1)):
         total = jnp.zeros(edge_in.shape[3:], F32)
         for dt in range(4):
@@ -380,11 +445,13 @@
     mail.finish()
 
 
-def forward(tokens, shift, scale, proj, fc1, fc2, gps, target):
+def forward(tokens, shift, scale, gate, projt, fc1, fc2t, lift, conv_a, conv_b, target):
     rows, width = tokens.shape
-    depth, hidden = fc1.shape
+    hidden = fc1.shape[1]
+    depth = (fc1.shape[0] + 15) // 16 * 16
     half = hidden // 2
-    n_out = proj.shape[1]
+    n_out = projt.shape[0]
+    wide = (depth, 2 * n_out)
     n_blk = 16
     height, breadth, ch = target.shape
     token_rows, n_cols = 4 * rows // 512, 128
@@ -398,20 +465,29 @@
             shape((2 * rows, half), BF16),
             shape((token_rows + 2, span, n_out), F32),
             shape((half, n_out), BF16),
-            shape(gps.shape[1:], F32),
+            shape(wide, F32),
             shape((n_blk, 2 * depth, 2 * rows), BF16),
+            shape((36, n_out, ch), BF16),
+            shape((3, 3 * ch, ch), BF16),
             shape((2, 2, breadth, ch), BF16),
             shape((2, height, LEAD, ch), BF16),
             shape((4, 2, LEAD, ch), BF16),
         ),
-        in_specs=[vmem] * 7 + [hbm],
-        out_specs=(hbm, hbm, vmem, vmem, vmem, hbm, hbm, hbm, hbm),
+        in_specs=[hbm] + [vmem] * 7 + [hbm] * 3,
+        out_specs=(hbm, hbm, vmem, vmem, vmem) + (hbm,) * 6,
         scratch_shapes=[
+            VMEM((depth, hidden), BF16),
+            VMEM((2,) + wide, F32),
             VMEM((rows, width), BF16),
+            VMEM((9, ch, ch), BF16),
+            VMEM((9, ch, ch), BF16),
+            VMEM((36, n_out, ch), BF16),
+            VMEM((3, 3 * ch, ch), BF16),
+            VMEM((2 * rows, width), BF16),
             VMEM((n_blk, 2 * rows, 2 * depth), BF16),
             VMEM((n_blk, 2 * depth, 2 * rows), BF16),
             VMEM((n_blk, 2 * depth, half), BF16),
-            VMEM(gps.shape[1:], F32),
+            VMEM(wide, F32),
             VMEM((hidden, 2 * n_out), F32),
             VMEM((half, 2 * n_out), F32),
             VMEM((half, 2 * n_out), F32),
@@ -430,44 +506,26 @@
             VMEM((2, 4, 1, span, 2 * n_out), F32),
             pltpu.SemaphoreType.DMA((72,)),
             pltpu.SemaphoreType.DMA((72,)),
-            pltpu.SemaphoreType.DMA((3,)),
+            pltpu.SemaphoreType.DMA((8,)),
         ],
         compiler_params=pltpu.CompilerParams(
-            collective_id=1, has_side_effects=True, vmem_limit_bytes=58 * 2**20
+            collective_id=1, has_side_effects=True, vmem_limit_bytes=60 * 2**20
         ),
-    )(tokens, shift, scale, proj, fc1, fc2, gps, target)
-
-
-def pixel_kernels(lift, conv_a):
-    lifted = {
-        (o, e): dot(lift, conv_a[3 * o + e])
-        for o in range(3)
-        for e in range(3)
-    }
-
-    def reach(pixel, cell):
-        return [o for o in range(3) if (pixel + o - 1) // 2 == cell]
-
-    out = {}
-    for r in range(-1, 5):
-        for c in range(-1, 5):
-            parts = []
-            for a in range(2):
-                for b in range(2):
-                    total = jnp.zeros_like(lifted[0, 0])
-                    for o in reach(r, a):
-                        for e in reach(c, b):
-                            total = total + lifted[o, e]
-                    parts.append(total)
-            out[r, c] = jnp.concatenate(parts, axis=0)
-    return out
+    )(tokens, shift, scale, gate, projt, fc1, fc2t, lift, conv_a, conv_b, target)
 
 
 def middle_kernel(
-    sums, lift, conv_a, conv_b, conv_bt, target, t_rows, t_cols, t_ends,
-    latent, lg,
-    patch, kern, f_ref, a_ref, b_ref, acc, want, gf, send, recv,
+    sums, *refs,
 ):
+    hbm, (latent, lg), refs = refs[:7], refs[7:9], refs[9:]
+    kern, target, t_rows, t_cols, t_ends, conv_b, conv_bt = refs[:7]
+    patch, f_ref, a_ref, b_ref, acc, want, gf, send, recv, local = refs[7:]
+    loads = [
+        pltpu.make_async_copy(src, dst, local.at[i])
+        for i, (src, dst) in enumerate(zip(hbm, refs))
+    ]
+    for load in loads:
+        load.start()
     grp, seq, tile = lax.axis_index("grp"), lax.axis_index("seq"), lax.axis_index("tile")
     core = seq % 2
 
@@ -481,10 +539,6 @@
     n_rows, here = n_tok - 2, span - 2 * EDGE
     pairs, ch = a_ref.shape[1], a_ref.shape[2] // 4
 
-    kernels = pixel_kernels(lift[...], conv_a)
-    for r in range(-1, 5):
-        for c in range(-1, 5):
-            kern[6 * (r + 1) + c + 1] = kernels[r, c].astype(BF16)
     height, breadth = target.shape[0], target.shape[1]
     body, lead = slice(LEAD, LEAD + breadth), slice(0, LEAD)
     trail = slice(LEAD + breadth, 2 * LEAD + breadth)
@@ -495,6 +549,8 @@
         want[rows, 0, at, :] = value[:, :, :128]
         want[rows, 1, at, :] = value[:, :, 128:]
 
+    for load in loads[1:5]:
+        load.wait()
     want_at(mid, body, target[...])
     want_at(slice(0, 2), body, t_rows[0])
     want_at(slice(2 + height, 4 + height), body, t_rows[1])
@@ -511,6 +567,8 @@
     for k in range(3):
         patch[k, 0] = jnp.zeros((span, width), BF16)
         patch[k, n_tok + 1] = jnp.zeros((span, width), BF16)
+
+    loads[0].wait()
 
     def near(phase):
         return [(d, phase - 4 * d) for d in (-1, 0, 1) if -1 <= phase - 4 * d <= 4]
@@ -566,6 +624,7 @@
                     value = term if value is None else value + term
                 acc[b, pl.ds(i * chunk, chunk)] = value.reshape(chunk, pairs, ch)
 
+    loads[5].wait()
     conv(a_ref, conv_b, height + 4, (height + 4) // 2)
 
     @pl.loop(0, height + 4)
@@ -576,6 +635,7 @@
             grad.append(jnp.where(inside(i - 2, b), diff, 0.0))
         spread(b_ref, i, *grad)
 
+    loads[6].wait()
     conv(b_ref, conv_bt, height + 2, (height + 2) // 2)
 
     @pl.loop(0, height + 2)
@@ -612,37 +672,41 @@
     mail.finish()
 
 
-def middle(sums, lift, conv_a, conv_b, conv_bt, target, t_rows, t_cols, t_ends):
+def middle(sums, kern, target, t_rows, t_cols, t_ends, conv_b, conv_bt):
     n_tok, span, width = sums.shape
     n_rows, here = n_tok - 2, span - 2 * EDGE
     height, breadth, ch = target.shape
     pairs = breadth // 2 + 2 * EDGE
-    vmem = pl.BlockSpec(memory_space=VMEM)
+    vmem, hbm = pl.BlockSpec(memory_space=VMEM), pl.BlockSpec(memory_space=pl.ANY)
     shape = jax.ShapeDtypeStruct
+    loaded = (kern, target, t_rows, t_cols, t_ends, conv_b, conv_bt)
     return pl.pallas_call(
         middle_kernel,
         out_shape=(
             shape((n_rows, here, width), F32),
             shape((2 * n_rows, 4 * here, width), BF16),
         ),
-        in_specs=[vmem] * 9,
+        in_specs=[vmem] + [hbm] * len(loaded),
         out_specs=(vmem,) * 2,
-        scratch_shapes=[
+        scratch_shapes=[VMEM(x.shape, x.dtype) for x in loaded]
+        + [
             VMEM((3, n_rows + 4, span, width), BF16),
-            VMEM((36, width, ch), BF16),
             VMEM((height + 8, 2, 2, 2 * span, ch // 2), F32),
             VMEM((height + 6, pairs, 4 * ch), BF16),
             VMEM((height + 4, pairs, 4 * ch), BF16),
             VMEM((2, height + 4, pairs, ch), F32),
             VMEM((height + 4, 2, breadth + 2 * LEAD, ch // 2), F32),
             VMEM((height + 2, 2, 2, pairs, ch // 2), F32),
-            pltpu.SemaphoreType.DMA((40,)),
-            pltpu.SemaphoreType.DMA((40,)),
+            pltpu.SemaphoreType.DMA((16,)),
+            pltpu.SemaphoreType.DMA((16,)),
+            pltpu.SemaphoreType.DMA((len(loaded),)),
         ],
         compiler_params=pltpu.CompilerParams(
             collective_id=3, has_side_effects=True, vmem_limit_bytes=58 * 2**20
         ),
-    )(sums, lift, conv_a, conv_b, conv_bt, target, t_rows, t_cols, t_ends)
+    )(sums, *loaded)
+
+
 def backward_kernel(
     nrmt_hbm, slope_hbm, act_hbm, fold, lg, gboth, out, two,
     nrmt, slope, act, gpre, st, sz_in, sy_out, sy_in, sfull, b_out, b_in, a_out, a_in, fin, fin_in,
@@ -745,9 +809,9 @@
     mail.arrived(s_ss, sfull.at[other], sibling)
     g_high, g_low = split(gboth[...])
     for h in range(2):
-        s_high, s_low = split(sfull[h].reshape(-1, half).T)
-        value = dot(s_high, g_high, NT) + dot(s_high, g_low, NT) + dot(s_low, g_high, NT)
-        two[h * half : (h + 1) * half, :] = value[:, : two.shape[1]]
+        s_high, s_low = split(sfull[h].reshape(-1, half))
+        value = dot(g_high, s_high) + dot(g_low, s_high) + dot(g_high, s_low)
+        two[:, h * half : (h + 1) * half] = value[: two.shape[0]]
 
     total = sum_b(0)
     for d in STEPS:
@@ -773,7 +837,7 @@
     shape = jax.ShapeDtypeStruct
     return pl.pallas_call(
         backward_kernel,
-        out_shape=(shape((here, 2 * half), F32), shape((2 * half, here), F32)),
+        out_shape=(shape((here, 2 * half), F32), shape((here, 2 * half), F32)),
         in_specs=[hbm] * 3 + [vmem] * 3,
         out_specs=(vmem,) * 2,
         scratch_shapes=[
@@ -802,48 +866,47 @@
     )(nrmt, slope, act, fold, lg, gboth)
 
 
+def leave_kernel(*refs):
+    for src, dst in zip(refs[:3], refs[3:]):
+        dst[...] = src[...]
+
+
+def leave(*values):
+    vmem = pl.BlockSpec(memory_space=VMEM)
+    return pl.pallas_call(
+        leave_kernel,
+        out_shape=tuple(jax.ShapeDtypeStruct(v.shape, v.dtype) for v in values),
+        in_specs=[vmem] * 3,
+        out_specs=(vmem,) * 3,
+    )(*values)
+
+
 def shards(tokens, shift, scale, gate, fc1, fc2, proj, lift, conv_a, conv_b, target):
     width = tokens.shape[3]
-    n_seq = lax.axis_size("seq")
-    seq, grp = lax.axis_index("seq"), lax.axis_index("grp")
     patch_width = proj.shape[1]
 
     cols_here = fc2.shape[1]
-    gps = []
-    for at in (grp, 1 - grp):
-        col_at = (at * n_seq + seq) * cols_here
-        gate_cols = lax.dynamic_slice_in_dim(gate[0], col_at, cols_here, 0)
-        proj_cols = lax.dynamic_slice_in_dim(proj, col_at, cols_here, 0)
-        here = gate_cols[:, None] * proj_cols.astype(F32)
-        zero = jnp.zeros_like(here)
-        pair = [jnp.where(grp == i, here, zero) for i in range(2)]
-        gps.append(jnp.concatenate(pair, axis=1))
-    gps = jnp.pad(jnp.stack(gps), ((0, 0), (0, 4), (0, 0)))
-
-    slope, act, sums, fold, gboth, nrmt, *borders = forward(
+    ch = conv_a.shape[2]
+    slope, act, sums, fold, gboth, nrmt, kern, conv_bt, *borders = forward(
         tokens[0].reshape(-1, width),
         shift,
         scale,
-        proj,
-        jnp.pad(fc1, ((0, 4), (0, 0))),
-        fc2,
-        gps,
+        gate,
+        proj.T,
+        fc1,
+        fc2.T,
+        lift,
+        conv_a.reshape(9, ch, ch),
+        conv_b.reshape(9, ch, ch),
         target[0],
     )
-    ch = conv_a.shape[2]
-    conv_bt = jnp.swapaxes(conv_b[::-1, ::-1], 2, 3).reshape(3, 3 * ch, ch)
     latent_mine, latent_rows = middle(
-        sums,
-        lift,
-        conv_a.reshape(9, ch, ch),
-        conv_b.reshape(3, 3 * ch, ch),
-        conv_bt,
-        target[0],
-        *borders,
+        sums, kern, target[0], *borders, conv_b.reshape(3, 3 * ch, ch), conv_bt
     )
     latent_rows = latent_rows.reshape(-1, patch_width)
     grad_one, grad_two = backward(nrmt, slope, act, fold, latent_rows, gboth, cols_here)
-    return (grad_one, grad_two, latent_mine[None])
+    grad_one, grad_two, latent_mine = leave(grad_one, grad_two, latent_mine)
+    return (grad_one, grad_two.T, latent_mine[None])
 
 
 def solution(mesh):

time: 133 us -> 120 us (0.902)
  local copies, waits for them, and re-layouts: 8.87 us -> 0 us
  Pallas kernels: 122 us -> 118 us
    pallas_call x1, Pallas kernels: 61.1 us -> 54.5 us  [forward(): pl.pallas_call(forward_kernel, out_shape=(shape((2 * rows, half), F32), s...]
    unnamed x17 -> x0, local copies, waits for them, and re-layouts: 5.74 us -> none
    pallas_call x0 -> x1, Pallas kernels: none -> 2.06 us  [leave(): pl.pallas_call(leave_kernel, out_shape=tuple((jax.ShapeDtypeStruct(v.shap...]
    transpose x2 -> x0, local copies, waits for them, and re-layouts: 1.6 us -> none  [shards(): conv_bt = jnp.swapaxes(conv_b[::-1, ::-1], 2, 3).reshape(3, 3 * ch, ch)]
where the time goes in v3:
time: 120 us; the launch traced here: 118 us
  Pallas kernels  118 us (98%)
    pallas_call x1, Pallas kernels, forward(): pl.pallas_call(forward_kernel, out_shape=(shape((2 * rows, half), F32), s...  54.5 us
    pallas_call x1, Pallas kernels, backward(): pl.pallas_call(backward_kernel, out_shape=(shape((here, 2 * half), F32),...  36.7 us
    pallas_call x1, Pallas kernels, middle(): pl.pallas_call(middle_kernel, out_shape=(shape((n_rows, here, width), F32...  24.4 us

profile of v3, /device:TPU:1, one launch (start us, length us, event | category | flops | bytes accessed | tf_op | source)
XLA Modules:
  0.0 118.3 jit_solution(12610473929772752670)
XLA Ops:
  0.6 54.5 %shard_map.130 = (f32[1024,640]{1,0:T(8,128)}, bf16[1024,640]{1,0:T(8,128)(2,1)}, f32[6,48,64]{2,1,0:T(8,128)}, bf16[640,64]{1,0:T(8,128)(2,1)}, f32[80,128]{1,0...) custom-call(bf16[512,2432]{1,0:T(8,128)(2,1)} %bitcast.14, ...), custom_call_target="tpu_custom_call" | custom-call | tf_op jit(solution)/shard_map/pallas_call | solution.py:461
  55.2 24.4 %shard_map.131 = (f32[4,32,64]{2,1,0:T(8,128)}, bf16[8,128,64]{2,1,0:T(8,128)(2,1)}) custom-call(f32[6,48,64]{2,1,0:T(8,128)} %get-tuple-element.25.sums, bf16[36,64,256]{2,1,0:T(8,128)(2,1)} %get-tuple-element.26.refs_0_, bf16[16,128,256]{2,1,0:T(8,128)(2,1)} %bitcast.13, bf16[2,2,128,256]{3,2,1,0:T(8,128)(2,1)} %get-tuple-element.27.refs_2_, ...), custom_call_target="tpu_custom_call" | custom-call | tf_op jit(solution)/shard_map/pallas_call | solution.py:683
  79.5 36.7 %shard_map.132 = (f32[76,1280]{1,0:T(8,128)}, f32[76,1280]{1,0:T(8,128)}) custom-call(bf16[16,160,1024]{2,1,0:T(8,128)(2,1)} %get-tuple-element.21.nrmt_hbm, f32[1024,640]{1,0:T(8,128)} %get-tuple-element.22.slope_hbm, bf16[1024,640]{1,0:T(8,128)(2,1)} %get-tuple-element.23.act_hbm, bf16[640,64]{1,0:T(8,128)(2,1)} %get-tuple-element.24.fold, ...), custom_call_target="tpu_custom_call" | custom-call | tf_op jit(solution)/shard_map/pallas_call | solution.py:838
  116.2 2.1 %shard_map.133 = (f32[76,1280]{1,0:T(8,128)}, f32[76,1280]{1,0:T(8,128)}, f32[4,32,64]{2,1,0:T(8,128)}) custom-call(f32[76,1280]{1,0:T(8,128)} %get-tuple-element.33.refs_0_, f32[76,1280]{1,0:T(8,128)} %get-tuple-element.34.refs_1_, f32[4,32,64]{2,1,0:T(8,128)} %get-tuple-element.35.refs_2_), custom_call_target="tpu_custom_call" | custom-call | tf_op jit(solution)/shard_map/pallas_call | solution.py:876

commit v4 on v3

--- a/solution.py
+++ b/solution.py
@@ -144,10 +144,10 @@
 
 
 def forward_kernel(
-    tokens_hbm, shift, scale, gate, projt, fc1_own, fc2t, lift, conv_a_hbm, conv_b_hbm, target,
+    tokens_hbm, shift, scale, gate, projt, fc1_own, fc2t, lift, conv_a_hbm, conv_b_hbm, target_hbm,
     slope_hbm, act_hbm, sums, fold, gboth, nrmt_hbm, kern_hbm, conv_bt_hbm,
-    t_rows, t_cols, t_ends,
-    fc1, gps, tokens, conv_a, conv_b, kern, conv_bt, normed, nrm, nrmt, gath, gin, wpart, wsib, wsum, wz_out, wz_in, wy_out, wy_in, wfull, xp,
+    want_hbm,
+    t_rows, t_cols, t_ends, want, target, fc1, gps, tokens, conv_a, conv_b, kern, conv_bt, normed, nrm, nrmt, gath, gin, wpart, wsib, wsum, wz_out, wz_in, wy_out, wy_in, wfull, xp,
     pre, act, part, part_in, psrc, main_in, edge_in, send, recv, local,
 ):
     y, z, core, device = place()
@@ -165,7 +165,12 @@
     loads = [
         pltpu.make_async_copy(src, dst, local.at[i])
         for i, (src, dst) in enumerate(
-            ((tokens_hbm, tokens), (conv_a_hbm, conv_a), (conv_b_hbm, conv_b))
+            (
+                (tokens_hbm, tokens),
+                (conv_a_hbm, conv_a),
+                (conv_b_hbm, conv_b),
+                (target_hbm, target),
+            )
         )
     ]
     for load in loads:
@@ -223,8 +228,7 @@
 
     loads[0].wait()
 
-    @pl.loop(0, here_rows // 64)
-    def _(i):
+    def normalise(i):
         x = tokens[pl.ds(pl.multiple_of(i * 64, 64), 64), :].astype(F32)
         center = x - jnp.mean(x, axis=1, keepdims=True)
         spread = jnp.mean(center * center, axis=1, keepdims=True)
@@ -232,6 +236,18 @@
         at = pl.ds(pl.multiple_of(core * here_rows + i * 64, 64), 64)
         normed[at, :] = value.astype(BF16)
 
+    s_b = mail.slots((da, d) for da in range(4) for d in STEPS)
+
+    def put_b(da):
+        ref = gath.at[block(da, 0)]
+        for d in STEPS:
+            mail.start(s_b[da, d], ref, ref, peer(0, d))
+
+    n_steps = here_rows // 64
+    pl.loop(0, n_steps // 2)(normalise)
+    mail.arrived(s_own, gath.at[own, theirs], sibling)
+    put_b(0)
+    pl.loop(n_steps // 2, n_steps)(normalise)
     blk_rows = pl.ds(pl.multiple_of(core * here_rows, 128), here_rows)
     s_n = mail.slot()
     mail.start(s_n, normed.at[blk_rows], normed.at[blk_rows], sibling)
@@ -245,7 +261,7 @@
     s_w = mail.slot()
     mail.start(s_w, wpart.at[pl.ds(pl.multiple_of(other * half, 16), half)], wsib, sibling)
 
-    def rechunk(i):
+    def window_of(i):
         first = 2 * cols * i // 128 * 128
         off = 2 * cols * i - first
         span = 256 if off + 2 * cols <= 256 else 384
@@ -254,9 +270,16 @@
         low_part = (k == r + off) & (r < cols)
         high_part = (k == r + (off + cols - rows)) & (r >= rows) & (r < rows + cols)
         pick = jnp.where(low_part | high_part, 1.0, 0.0).astype(BF16)
-        value = normed[:, first : first + span]
+        return normed[:, first : first + span], pick
+
+    def rechunk(i):
+        value, pick = window_of(i)
         nrm[i] = dot(value, pick, NT).astype(BF16)
-        nrmt[i] = dot(pick, value, NT).astype(BF16)
+
+    def rechunk_turned(indices):
+        for i in indices:
+            value, pick = window_of(i)
+            nrmt[i] = dot(pick, value, NT).astype(BF16)
 
     mail.arrived(s_w, wsib, sibling)
     wsum[...] = wpart[pl.ds(pl.multiple_of(core * half, 16), half), :] + wsib[...]
@@ -267,18 +290,8 @@
         src = wz_out.at[pl.ds(pl.multiple_of(to * wq, 16), wq)]
         mail.start(s_wz[d], src, wz_in.at[d - 1], device(y, to, core))
 
-    s_b = mail.slots((da, d) for da in range(4) for d in STEPS)
-
-    def put_b(da):
-        ref = gath.at[block(da, 0)]
-        for d in STEPS:
-            mail.start(s_b[da, d], ref, ref, peer(0, d))
-
-    mail.arrived(s_own, gath.at[own, theirs], sibling)
-    put_b(0)
-
     keep = [
-        pltpu.make_async_copy(src, dst, local.at[3 + i])
+        pltpu.make_async_copy(src, dst, local.at[4 + i])
         for i, (src, dst) in enumerate(
             (
                 (nrmt, nrmt_hbm),
@@ -286,6 +299,7 @@
                 (pre, slope_hbm),
                 (kern, kern_hbm),
                 (conv_bt, conv_bt_hbm),
+                (want, want_hbm),
             )
         )
     ]
@@ -294,13 +308,6 @@
     for i, value in enumerate(kernels.values()):
         kern[i] = value.astype(BF16)
     keep[3].start()
-    loads[2].wait()
-    ch = conv_b.shape[2]
-    for o in range(3):
-        for e in range(3):
-            conv_bt[o, e * ch : (e + 1) * ch, :] = conv_b[8 - 3 * o - e].T
-    keep[4].start()
-    xp[...] = dot(tokens[...], projt[...], NT).reshape(xp.shape)
 
     def relay(d):
         at = block(-d, 0)
@@ -333,15 +340,14 @@
         for d in STEPS:
             mail.start(s_wa[d], wfull.at[at], wfull.at[at], device(y, (z + d) % 4, core))
 
-    w_along_y()
     relay(1)
     relay(3)
-    w_back()
-    relay(2)
+    w_along_y()
     mail.arrived(s_n, normed.at[pl.ds(pl.multiple_of(other * here_rows, 128), here_rows)], sibling)
     for i in range(gath.shape[0]):
         rechunk(i)
-    keep[0].start()
+    relay(2)
+    loads[3].wait()
     height, breadth = target.shape[0], target.shape[1]
     top_rows, end_rows = pl.ds(0, 2), pl.ds(height - 2, 2)
     lead, trail = pl.ds(0, LEAD), pl.ds(breadth - LEAD, LEAD)
@@ -378,6 +384,18 @@
         multiply([(da, 3), (da, 1)])
         take_b(da, 2)
         multiply([(da, 2)])
+        if da == 0:
+            rechunk_turned(range(0, 5))
+            w_back()
+        elif da == 3:
+            rechunk_turned(range(5, 8))
+            loads[2].wait()
+            ch = conv_b.shape[2]
+            for o in range(3):
+                for e in range(3):
+                    conv_bt[o, e * ch : (e + 1) * ch, :] = conv_b[8 - 3 * o - e].T
+            keep[4].start()
+            xp[...] = dot(tokens[...], projt[...], NT).reshape(xp.shape)
 
     for d in STEPS:
         frm = (z + 4 - d) % 4
@@ -422,6 +440,28 @@
         mail.start(s_around[ds, dt], src, dst, tile_peer(ds, dt))
     pre[...] = gelu_slope(pre[...])
     keep[2].start()
+    rechunk_turned(range(8, 16))
+    keep[0].start()
+
+    for ds, dt in NEXT:
+        mail.arrived(s_border[ds, dt], borders[ds, dt][1], tile_peer(-ds, -dt))
+    body, first_cols = slice(LEAD, LEAD + breadth), slice(0, LEAD)
+    last_cols = slice(LEAD + breadth, 2 * LEAD + breadth)
+    inner, under = slice(2, 2 + height), slice(2 + height, 4 + height)
+
+    def want_at(rows, at, value):
+        value = value.astype(F32)
+        want[rows, 0, at, :] = value[:, :, :128]
+        want[rows, 1, at, :] = value[:, :, 128:]
+
+    want_at(inner, body, target[...])
+    want_at(slice(0, 2), body, t_rows[0])
+    want_at(under, body, t_rows[1])
+    for side, at in ((0, first_cols), (1, last_cols)):
+        want_at(inner, at, t_cols[side])
+        want_at(slice(0, 2), at, t_ends[side])
+        want_at(under, at, t_ends[2 + side])
+    keep[5].start()
 
     total = psrc[:, window(0), :]
     for dt in range(1, 4):
@@ -438,8 +478,6 @@
         total = total[:, n_out:] if i == 0 else total[:, :n_out]
         sums[(n_rows + 1) * i] = jnp.where(outside, 0.0, total)
 
-    for ds, dt in NEXT:
-        mail.arrived(s_border[ds, dt], borders[ds, dt][1], tile_peer(-ds, -dt))
     for copy in keep:
         copy.wait()
     mail.finish()
@@ -469,13 +507,16 @@
             shape((n_blk, 2 * depth, 2 * rows), BF16),
             shape((36, n_out, ch), BF16),
             shape((3, 3 * ch, ch), BF16),
-            shape((2, 2, breadth, ch), BF16),
-            shape((2, height, LEAD, ch), BF16),
-            shape((4, 2, LEAD, ch), BF16),
+            shape((height + 4, 2, breadth + 2 * LEAD, ch // 2), F32),
         ),
         in_specs=[hbm] + [vmem] * 7 + [hbm] * 3,
-        out_specs=(hbm, hbm, vmem, vmem, vmem) + (hbm,) * 6,
+        out_specs=(hbm, hbm, vmem, vmem, vmem) + (hbm,) * 4,
         scratch_shapes=[
+            VMEM((2, 2, breadth, ch), BF16),
+            VMEM((2, height, LEAD, ch), BF16),
+            VMEM((4, 2, LEAD, ch), BF16),
+            VMEM((height + 4, 2, breadth + 2 * LEAD, ch // 2), F32),
+            VMEM((height, breadth, ch), BF16),
             VMEM((depth, hidden), BF16),
             VMEM((2,) + wide, F32),
             VMEM((rows, width), BF16),
@@ -506,7 +547,7 @@
             VMEM((2, 4, 1, span, 2 * n_out), F32),
             pltpu.SemaphoreType.DMA((72,)),
             pltpu.SemaphoreType.DMA((72,)),
-            pltpu.SemaphoreType.DMA((8,)),
+            pltpu.SemaphoreType.DMA((10,)),
         ],
         compiler_params=pltpu.CompilerParams(
             collective_id=1, has_side_effects=True, vmem_limit_bytes=60 * 2**20
@@ -517,9 +558,9 @@
 def middle_kernel(
     sums, *refs,
 ):
-    hbm, (latent, lg), refs = refs[:7], refs[7:9], refs[9:]
-    kern, target, t_rows, t_cols, t_ends, conv_b, conv_bt = refs[:7]
-    patch, f_ref, a_ref, b_ref, acc, want, gf, send, recv, local = refs[7:]
+    hbm, (latent, lg), refs = refs[:4], refs[4:6], refs[6:]
+    kern, want, conv_b, conv_bt = refs[:4]
+    patch, f_ref, a_ref, b_ref, acc, gf, send, recv, local = refs[4:]
     loads = [
         pltpu.make_async_copy(src, dst, local.at[i])
         for i, (src, dst) in enumerate(zip(hbm, refs))
@@ -539,27 +580,8 @@
     n_rows, here = n_tok - 2, span - 2 * EDGE
     pairs, ch = a_ref.shape[1], a_ref.shape[2] // 4
 
-    height, breadth = target.shape[0], target.shape[1]
-    body, lead = slice(LEAD, LEAD + breadth), slice(0, LEAD)
-    trail = slice(LEAD + breadth, 2 * LEAD + breadth)
-    mid = slice(2, 2 + height)
-
-    def want_at(rows, at, value):
-        value = value.astype(F32)
-        want[rows, 0, at, :] = value[:, :, :128]
-        want[rows, 1, at, :] = value[:, :, 128:]
-
-    for load in loads[1:5]:
-        load.wait()
-    want_at(mid, body, target[...])
-    want_at(slice(0, 2), body, t_rows[0])
-    want_at(slice(2 + height, 4 + height), body, t_rows[1])
-    for side, at in ((0, lead), (1, trail)):
-        want_at(mid, at, t_cols[side])
-        want_at(slice(0, 2), at, t_ends[side])
-        want_at(slice(2 + height, 4 + height), at, t_ends[2 + side])
-
     rows = {r: sums[r] for r in range(n_tok)}
+    height, breadth = f_ref.shape[0] - 8, 4 * here
     for r in range(n_tok):
         patch[0, r + 1] = pltpu.roll(rows[r], 1, 0).astype(BF16)
         patch[1, r + 1] = rows[r].astype(BF16)
@@ -624,8 +646,9 @@
                     value = term if value is None else value + term
                 acc[b, pl.ds(i * chunk, chunk)] = value.reshape(chunk, pairs, ch)
 
-    loads[5].wait()
+    loads[2].wait()
     conv(a_ref, conv_b, height + 4, (height + 4) // 2)
+    loads[1].wait()
 
     @pl.loop(0, height + 4)
     def _(i):
@@ -635,7 +658,7 @@
             grad.append(jnp.where(inside(i - 2, b), diff, 0.0))
         spread(b_ref, i, *grad)
 
-    loads[6].wait()
+    loads[3].wait()
     conv(b_ref, conv_bt, height + 2, (height + 2) // 2)
 
     @pl.loop(0, height + 2)
@@ -672,14 +695,14 @@
     mail.finish()
 
 
-def middle(sums, kern, target, t_rows, t_cols, t_ends, conv_b, conv_bt):
+def middle(sums, kern, want, conv_b, conv_bt):
     n_tok, span, width = sums.shape
     n_rows, here = n_tok - 2, span - 2 * EDGE
-    height, breadth, ch = target.shape
+    height, breadth, ch = want.shape[0] - 4, 4 * here, conv_bt.shape[2]
     pairs = breadth // 2 + 2 * EDGE
     vmem, hbm = pl.BlockSpec(memory_space=VMEM), pl.BlockSpec(memory_space=pl.ANY)
     shape = jax.ShapeDtypeStruct
-    loaded = (kern, target, t_rows, t_cols, t_ends, conv_b, conv_bt)
+    loaded = (kern, want, conv_b, conv_bt)
     return pl.pallas_call(
         middle_kernel,
         out_shape=(
@@ -695,7 +718,6 @@
             VMEM((height + 6, pairs, 4 * ch), BF16),
             VMEM((height + 4, pairs, 4 * ch), BF16),
             VMEM((2, height + 4, pairs, ch), F32),
-            VMEM((height + 4, 2, breadth + 2 * LEAD, ch // 2), F32),
             VMEM((height + 2, 2, 2, pairs, ch // 2), F32),
             pltpu.SemaphoreType.DMA((16,)),
             pltpu.SemaphoreType.DMA((16,)),
@@ -764,13 +786,13 @@
         mail.start(s_a[d], a_out.at[d - 1], a_in.at[d - 1], peer(d, 0))
 
     loads[0].wait()
-    st[...] = dot(lg[...], act[...], TN)
+    st[...] = dot(lg[...], act[...], TN).astype(BF16)
     sq = st.shape[0] // 4
     s_sz, s_sy, s_sa = mail.slots(STEPS), mail.slots(STEPS), mail.slots(STEPS)
     await_peers(peers)
     for d in STEPS:
         to = (z + d) % 4
-        src = st.at[pl.ds(pl.multiple_of(to * sq, 8), sq)]
+        src = st.at[pl.ds(pl.multiple_of(to * sq, 16), sq)]
         mail.start(s_sz[d], src, sz_in.at[d - 1], device(y, to, core))
 
     loads[1].wait()
@@ -780,16 +802,19 @@
 
     for d in STEPS:
         mail.arrived(s_sz[d], sz_in.at[d - 1], device(y, (z + 4 - d) % 4, core))
-    s_at = pl.ds(pl.multiple_of(z * sq, 8), sq)
-    sy_out[...] = st[s_at, :] + sz_in[0] + sz_in[1] + sz_in[2]
+    s_at = pl.ds(pl.multiple_of(z * sq, 16), sq)
+    total = st[s_at, :].astype(F32)
+    for d in STEPS:
+        total = total + sz_in[d - 1].astype(F32)
+    sy_out[...] = total.astype(BF16)
     for d in STEPS:
         mail.start(s_sy[d], sy_out, sy_in.at[d - 1], device((y + d) % 4, z, core))
 
     send_b(1)
     for d in STEPS:
         mail.arrived(s_sy[d], sy_in.at[d - 1], device((y + 4 - d) % 4, z, core))
-    sfull[core, grp, s_at] = sy_out[...] + sy_in[1]
-    sfull[core, 1 - grp, s_at] = sy_in[0] + sy_in[2]
+    sfull[core, grp, s_at] = (total + sy_in[1].astype(F32)).astype(BF16)
+    sfull[core, 1 - grp, s_at] = (sy_in[0].astype(F32) + sy_in[2].astype(F32)).astype(BF16)
     for d in STEPS:
         ref = sfull.at[core, :, s_at]
         mail.start(s_sa[d], ref, ref, device(y, (z + d) % 4, core))
@@ -799,7 +824,7 @@
     send_a(2)
     for d in STEPS:
         frm = (z + 4 - d) % 4
-        at = pl.ds(pl.multiple_of(frm * sq, 8), sq)
+        at = pl.ds(pl.multiple_of(frm * sq, 16), sq)
         mail.arrived(s_sa[d], sfull.at[core, :, at], device(y, frm, core))
     s_ss = mail.slot()
     mail.start(s_ss, sfull.at[core], sfull.at[core], sibling)
@@ -809,8 +834,8 @@
     mail.arrived(s_ss, sfull.at[other], sibling)
     g_high, g_low = split(gboth[...])
     for h in range(2):
-        s_high, s_low = split(sfull[h].reshape(-1, half))
-        value = dot(g_high, s_high) + dot(g_low, s_high) + dot(g_high, s_low)
+        sums = sfull[h].reshape(-1, half)
+        value = dot(g_high, sums) + dot(g_low, sums)
         two[:, h * half : (h + 1) * half] = value[: two.shape[0]]
 
     total = sum_b(0)
@@ -845,11 +870,11 @@
             VMEM(slope.shape, F32),
             VMEM(act.shape, BF16),
             VMEM((rows, half), BF16),
-            VMEM((width, half), F32),
-            VMEM((3, width // 4, half), F32),
-            VMEM((width // 4, half), F32),
-            VMEM((3, width // 4, half), F32),
-            VMEM((2, 2, width, half), F32),
+            VMEM((width, half), BF16),
+            VMEM((3, width // 4, half), BF16),
+            VMEM((width // 4, half), BF16),
+            VMEM((3, width // 4, half), BF16),
+            VMEM((2, 2, width, half), BF16),
             VMEM((4, 3, depth, half), BF16),
             VMEM((4, 3, depth, half), BF16),
             VMEM((3, depth, half), BF16),
@@ -887,7 +912,7 @@
 
     cols_here = fc2.shape[1]
     ch = conv_a.shape[2]
-    slope, act, sums, fold, gboth, nrmt, kern, conv_bt, *borders = forward(
+    slope, act, sums, fold, gboth, nrmt, kern, conv_bt, want = forward(
         tokens[0].reshape(-1, width),
         shift,
         scale,
@@ -901,7 +926,7 @@
         target[0],
     )
     latent_mine, latent_rows = middle(
-        sums, kern, target[0], *borders, conv_b.reshape(3, 3 * ch, ch), conv_bt
+        sums, kern, want, conv_b.reshape(3, 3 * ch, ch), conv_bt
     )
     latent_rows = latent_rows.reshape(-1, patch_width)
     grad_one, grad_two = backward(nrmt, slope, act, fold, latent_rows, gboth, cols_here)

time: 120 us -> 116 us (0.967)
  Pallas kernels: 118 us -> 115 us
    pallas_call x1, Pallas kernels: 36.7 us -> 35.3 us  [backward(): pl.pallas_call(backward_kernel, out_shape=(shape((here, 2 * half), F32),...]
where the time goes in v4:
time: 116 us; the launch traced here: 115 us
  Pallas kernels  115 us (99%)
    pallas_call x1, Pallas kernels, forward(): pl.pallas_call(forward_kernel, out_shape=(shape((2 * rows, half), F32), s...  53.4 us
    pallas_call x1, Pallas kernels, backward(): pl.pallas_call(backward_kernel, out_shape=(shape((here, 2 * half), F32),...  35.3 us
    pallas_call x1, Pallas kernels, middle(): pl.pallas_call(middle_kernel, out_shape=(shape((n_rows, here, width), F32...  24 us

profile of v4, /device:TPU:1, one launch (start us, length us, event | category | flops | bytes accessed | tf_op | source)
XLA Modules:
  0.0 115.4 jit_solution(10996699983072731530)
XLA Ops:
  0.6 53.4 %shard_map.130 = (f32[1024,640]{1,0:T(8,128)}, bf16[1024,640]{1,0:T(8,128)(2,1)}, f32[6,48,64]{2,1,0:T(8,128)}, bf16[640,64]{1,0:T(8,128)(2,1)}, f32[80,128]{1,0...) custom-call(bf16[512,2432]{1,0:T(8,128)(2,1)} %bitcast.12, ...), custom_call_target="tpu_custom_call" | custom-call | tf_op jit(solution)/shard_map/pallas_call | solution.py:499
  54.1 24.0 %shard_map.131 = (f32[4,32,64]{2,1,0:T(8,128)}, bf16[8,128,64]{2,1,0:T(8,128)(2,1)}) custom-call(f32[6,48,64]{2,1,0:T(8,128)} %get-tuple-element.23.sums, bf16[36,64,256]{2,1,0:T(8,128)(2,1)} %get-tuple-element.24.refs_0_, f32[20,2,160,128]{3,2,1,0:T(8,128)} %get-tuple-element.25.refs_1_, bf16[3,768,256]{2,1,0:T(8,128)(2,1)} %bitcast.11, ...), custom_call_target="tpu_custom_call" | custom-call | tf_op jit(solution)/shard_map/pallas_call | solution.py:706
  78.0 35.3 %shard_map.132 = (f32[76,1280]{1,0:T(8,128)}, f32[76,1280]{1,0:T(8,128)}) custom-call(bf16[16,160,1024]{2,1,0:T(8,128)(2,1)} %get-tuple-element.19.nrmt_hbm, f32[1024,640]{1,0:T(8,128)} %get-tuple-element.20.slope_hbm, bf16[1024,640]{1,0:T(8,128)(2,1)} %get-tuple-element.21.act_hbm, bf16[640,64]{1,0:T(8,128)(2,1)} %get-tuple-element.22.fold, ...), custom_call_target="tpu_custom_call" | custom-call | tf_op jit(solution)/shard_map/pallas_call | solution.py:863
  113.4 2.1 %shard_map.133 = (f32[76,1280]{1,0:T(8,128)}, f32[76,1280]{1,0:T(8,128)}, f32[4,32,64]{2,1,0:T(8,128)}) custom-call(f32[76,1280]{1,0:T(8,128)} %get-tuple-element.29.refs_0_, f32[76,1280]{1,0:T(8,128)} %get-tuple-element.30.refs_1_, f32[4,32,64]{2,1,0:T(8,128)} %get-tuple-element.31.refs_2_), custom_call_target="tpu_custom_call" | custom-call | tf_op jit(solution)/shard_map/pallas_call | solution.py:901

commit v5 on v4

--- a/solution.py
+++ b/solution.py
@@ -12,6 +12,7 @@
 NT = (((1,), (1,)), ((), ()))
 TN = (((0,), (0,)), ((), ()))
 EDGE = 8
+PAIR_EDGE = 4
 LEAD = 16
 NEXT = [(1, 0), (-1, 0), (0, 1), (0, -1), (1, 1), (1, -1), (-1, 1), (-1, -1)]
 AROUND = [(0, 1), (0, 2), (0, 3)] + [(ds, dt) for ds in (-1, 1) for dt in range(4)]
@@ -320,25 +321,28 @@
     def w_along_y():
         for d in STEPS:
             mail.arrived(s_wz[d], wz_in.at[d - 1], device(y, (z + 4 - d) % 4, core))
-        here = pl.ds(pl.multiple_of(z * wq, 16), wq)
-        total = wsum[here, :]
+        total = wsum[pl.ds(pl.multiple_of(z * wq, 16), wq), :]
         for d in STEPS:
             total = total + wz_in[d - 1].astype(F32)
-        wsum[here, :] = total
-        wy_out[...] = total.astype(BF16)
+        for i in range(2):
+            image = total[:, i * n_out : (i + 1) * n_out]
+            wy_out[i] = jnp.concatenate([image[: wq // 2], image[wq // 2 :]], axis=1).astype(BF16)
         for d in STEPS:
-            mail.start(s_wy[d], wy_out, wy_in.at[d - 1], device((y + d) % 4, z, core))
+            src = wy_out.at[(grp + d) % 2]
+            mail.start(s_wy[d], src, wy_in.at[d - 1], device((y + d) % 4, z, core))
+
+    def w_rows(z):
+        return pl.ds(pl.multiple_of(z * (wq // 2), 16), wq // 2)
 
     def w_back():
+        total = wy_out[grp].astype(F32)
         for d in STEPS:
             mail.arrived(s_wy[d], wy_in.at[d - 1], device((y + 4 - d) % 4, z, core))
-        at = pl.ds(pl.multiple_of(z * wq, 16), wq)
-        total = wsum[at, :]
+            total = total + wy_in[d - 1].astype(F32)
+        wfull[w_rows(z), :] = total.astype(BF16)
         for d in STEPS:
-            total = total + wy_in[d - 1].astype(F32)
-        wfull[at, :] = total.astype(BF16)
-        for d in STEPS:
-            mail.start(s_wa[d], wfull.at[at], wfull.at[at], device(y, (z + d) % 4, core))
+            ref = wfull.at[w_rows(z)]
+            mail.start(s_wa[d], ref, ref, device(y, (z + d) % 4, core))
 
     relay(1)
     relay(3)
@@ -385,10 +389,10 @@
         take_b(da, 2)
         multiply([(da, 2)])
         if da == 0:
-            rechunk_turned(range(0, 5))
+            rechunk_turned(range(0, 6))
             w_back()
         elif da == 3:
-            rechunk_turned(range(5, 8))
+            rechunk_turned(range(6, 11))
             loads[2].wait()
             ch = conv_b.shape[2]
             for o in range(3):
@@ -396,12 +400,17 @@
                     conv_bt[o, e * ch : (e + 1) * ch, :] = conv_b[8 - 3 * o - e].T
             keep[4].start()
             xp[...] = dot(tokens[...], projt[...], NT).reshape(xp.shape)
+        elif da == 1:
+            rechunk_turned(range(11, 16))
+            keep[0].start()
 
     for d in STEPS:
         frm = (z + 4 - d) % 4
-        at = pl.ds(pl.multiple_of(frm * wq, 16), wq)
-        mail.arrived(s_wa[d], wfull.at[at], device(y, frm, core))
-    fold[...] = jnp.where(grp == 0, wfull[:, :n_out], wfull[:, n_out:])
+        mail.arrived(s_wa[d], wfull.at[w_rows(frm)], device(y, frm, core))
+    for i in range(4):
+        value = wfull[i * (wq // 2) : (i + 1) * (wq // 2), :]
+        fold[i * wq : i * wq + wq // 2, :] = value[:, :n_out]
+        fold[i * wq + wq // 2 : (i + 1) * wq, :] = value[:, n_out:]
 
     n_rows, n_cols = xp.shape[0], xp.shape[1]
     s_part = mail.slot()
@@ -440,8 +449,6 @@
         mail.start(s_around[ds, dt], src, dst, tile_peer(ds, dt))
     pre[...] = gelu_slope(pre[...])
     keep[2].start()
-    rechunk_turned(range(8, 16))
-    keep[0].start()
 
     for ds, dt in NEXT:
         mail.arrived(s_border[ds, dt], borders[ds, dt][1], tile_peer(-ds, -dt))
@@ -534,9 +541,9 @@
             VMEM((half, 2 * n_out), F32),
             VMEM((half, 2 * n_out), BF16),
             VMEM((3, half // 4, 2 * n_out), BF16),
-            VMEM((half // 4, 2 * n_out), BF16),
-            VMEM((3, half // 4, 2 * n_out), BF16),
-            VMEM((half, 2 * n_out), BF16),
+            VMEM((2, half // 8, 2 * n_out), BF16),
+            VMEM((3, half // 8, 2 * n_out), BF16),
+            VMEM((half // 2, 2 * n_out), BF16),
             VMEM((token_rows, n_cols, n_out), F32),
             VMEM((2 * rows, half), F32),
             VMEM((2 * rows, half), BF16),
@@ -609,9 +616,11 @@
                 f_ref[4 * tr + al, ph % 2, 0, at, :] = value[tr, :, :128]
                 f_ref[4 * tr + al, ph % 2, 1, at, :] = value[tr, :, 128:]
 
+    first_pair = 2 * EDGE - PAIR_EDGE
+
     def inside(row, b):
         r = seq * height + row
-        c = 2 * (tile * breadth // 2 + lax.broadcasted_iota(jnp.int32, (pairs, 1), 0) - EDGE) + b
+        c = 2 * (tile * breadth // 2 + lax.broadcasted_iota(jnp.int32, (pairs, 1), 0) - PAIR_EDGE) + b
         return (r >= 0) & (r < 16 * height) & (c >= 0) & (c < 4 * breadth)
 
     def both(ref, at, rows):
@@ -627,12 +636,12 @@
     def _(i):
         smooth = []
         for b in range(2):
-            f = both(f_ref, (i + 1, b), slice(EDGE, EDGE + pairs))
+            f = both(f_ref, (i + 1, b), slice(first_pair, first_pair + pairs))
             sigma = jax.nn.sigmoid(f)
             smooth.append(jnp.where(inside(i - 3, b), f * sigma, 0.0))
             slope = sigma * (1.0 + f * (1.0 - sigma))
-            f_ref[i + 1, b, 0, EDGE : EDGE + pairs, :] = slope[:, :128]
-            f_ref[i + 1, b, 1, EDGE : EDGE + pairs, :] = slope[:, 128:]
+            f_ref[i + 1, b, 0, first_pair : first_pair + pairs, :] = slope[:, :128]
+            f_ref[i + 1, b, 1, first_pair : first_pair + pairs, :] = slope[:, 128:]
         spread(a_ref, i, *smooth)
 
     def conv(src, weights, out_rows, chunk):
@@ -654,7 +663,7 @@
     def _(i):
         grad = []
         for b in range(2):
-            diff = acc[b, i] - both(want, (i,), pl.ds(b, pairs, stride=2))
+            diff = acc[b, i] - both(want, (i,), pl.ds(LEAD - 2 * PAIR_EDGE + b, pairs, stride=2))
             grad.append(jnp.where(inside(i - 2, b), diff, 0.0))
         spread(b_ref, i, *grad)
 
@@ -664,14 +673,14 @@
     @pl.loop(0, height + 2)
     def _(i):
         for b in range(2):
-            value = acc[b, i] * both(f_ref, (i + 3, b), slice(EDGE, EDGE + pairs))
+            value = acc[b, i] * both(f_ref, (i + 3, b), slice(first_pair, first_pair + pairs))
             value = jnp.where(inside(i - 1, b), value, 0.0)
             gf[i, b, 0], gf[i, b, 1] = value[:, :128], value[:, 128:]
 
     grad = None
     for r in range(-1, 5):
         for c in range(-1, 5):
-            at = pl.ds(EDGE + c // 2, here, stride=2)
+            at = pl.ds(PAIR_EDGE + c // 2, here, stride=2)
             lhs = jnp.concatenate(
                 [both(gf, (4 * tr + r + 1, c % 2), at).astype(BF16) for tr in range(n_rows)],
                 axis=0,
@@ -699,7 +708,7 @@
     n_tok, span, width = sums.shape
     n_rows, here = n_tok - 2, span - 2 * EDGE
     height, breadth, ch = want.shape[0] - 4, 4 * here, conv_bt.shape[2]
-    pairs = breadth // 2 + 2 * EDGE
+    pairs = breadth // 2 + 2 * PAIR_EDGE
     vmem, hbm = pl.BlockSpec(memory_space=VMEM), pl.BlockSpec(memory_space=pl.ANY)
     shape = jax.ShapeDtypeStruct
     loaded = (kern, want, conv_b, conv_bt)

time: 116 us -> 115 us (level)
  no operation moved by 1% of the time
where the time goes in v5:
time: 115 us; the launch traced here: 114 us
  Pallas kernels  114 us (99%)
    pallas_call x1, Pallas kernels, forward(): pl.pallas_call(forward_kernel, out_shape=(shape((2 * rows, half), F32), s...  53.4 us
    pallas_call x1, Pallas kernels, backward(): pl.pallas_call(backward_kernel, out_shape=(shape((here, 2 * half), F32),...  35 us
    pallas_call x1, Pallas kernels, middle(): pl.pallas_call(middle_kernel, out_shape=(shape((n_rows, here, width), F32...  23.2 us

profile of v5, /device:TPU:1, one launch (start us, length us, event | category | flops | bytes accessed | tf_op | source)
XLA Modules:
  0.0 114.4 jit_solution(14711733761040217510)
XLA Ops:
  0.6 53.4 %shard_map.130 = (f32[1024,640]{1,0:T(8,128)}, bf16[1024,640]{1,0:T(8,128)(2,1)}, f32[6,48,64]{2,1,0:T(8,128)}, bf16[640,64]{1,0:T(8,128)(2,1)}, f32[80,128]{1,0...) custom-call(bf16[512,2432]{1,0:T(8,128)(2,1)} %bitcast.12, ...), custom_call_target="tpu_custom_call" | custom-call | tf_op jit(solution)/shard_map/pallas_call | solution.py:506
  54.1 23.2 %shard_map.131 = (f32[4,32,64]{2,1,0:T(8,128)}, bf16[8,128,64]{2,1,0:T(8,128)(2,1)}) custom-call(f32[6,48,64]{2,1,0:T(8,128)} %get-tuple-element.23.sums, bf16[36,64,256]{2,1,0:T(8,128)(2,1)} %get-tuple-element.24.refs_0_, f32[20,2,160,128]{3,2,1,0:T(8,128)} %get-tuple-element.25.refs_1_, bf16[3,768,256]{2,1,0:T(8,128)(2,1)} %bitcast.11, ...), custom_call_target="tpu_custom_call" | custom-call | tf_op jit(solution)/shard_map/pallas_call | solution.py:715
  77.3 35.0 %shard_map.132 = (f32[76,1280]{1,0:T(8,128)}, f32[76,1280]{1,0:T(8,128)}) custom-call(bf16[16,160,1024]{2,1,0:T(8,128)(2,1)} %get-tuple-element.19.nrmt_hbm, f32[1024,640]{1,0:T(8,128)} %get-tuple-element.20.slope_hbm, bf16[1024,640]{1,0:T(8,128)(2,1)} %get-tuple-element.21.act_hbm, bf16[640,64]{1,0:T(8,128)(2,1)} %get-tuple-element.22.fold, ...), custom_call_target="tpu_custom_call" | custom-call | tf_op jit(solution)/shard_map/pallas_call | solution.py:872
  112.3 2.1 %shard_map.133 = (f32[76,1280]{1,0:T(8,128)}, f32[76,1280]{1,0:T(8,128)}, f32[4,32,64]{2,1,0:T(8,128)}) custom-call(f32[76,1280]{1,0:T(8,128)} %get-tuple-element.29.refs_0_, f32[76,1280]{1,0:T(8,128)} %get-tuple-element.30.refs_1_, f32[4,32,64]{2,1,0:T(8,128)} %get-tuple-element.31.refs_2_), custom_call_target="tpu_custom_call" | custom-call | tf_op jit(solution)/shard_map/pallas_call | solution.py:910

commit v6 on v5

--- a/solution.py
+++ b/solution.py
@@ -187,6 +187,29 @@
     )
     fc1[last:] = tail.astype(BF16)
 
+    await_peers(peers)
+
+    def peer(da, db):
+        return device(*turn((a + da) % 4, (b + db) % 4), core)
+
+    def block(da, db):
+        return block_of(*turn((a + da) % 4, (b + db) % 4))
+
+    own = block(0, 0)
+    mine = pl.ds(pl.multiple_of(core * rows, 16), rows)
+    theirs = pl.ds(pl.multiple_of(other * rows, 16), rows)
+    s_a = mail.slots((h, d) for h in range(2) for d in STEPS)
+    r_a = {d: mail.slot(2) for d in STEPS}
+    s_gate, s_own = mail.slot(), mail.slot()
+    src = fc1.at[:, pl.ds(pl.multiple_of(other * half, 128), half)]
+    mail.start(s_own, src, gath.at[own, mine], sibling)
+    for d in STEPS:
+        for h in range(2):
+            to = device((y + d) % 4, z, 0) if h == 0 else device(y, (z + d) % 4, 1)
+            src = fc1.at[:, h * half : (h + 1) * half]
+            mail.start(s_a[h, d], src, gath.at[own, mine], to, r_a[d] + core)
+    gath[own, mine, :] = fc1[:, pl.ds(pl.multiple_of(core * half, 128), half)]
+
     n_out = projt.shape[0]
     seq = lax.axis_index("seq")
     for i, g in enumerate((grp, 1 - grp)):
@@ -202,30 +225,8 @@
         gps[i] = jnp.concatenate(
             [jnp.where(grp == 0, value, zero), jnp.where(grp == 1, value, zero)], axis=1
         )
-    await_peers(peers)
-
-    def peer(da, db):
-        return device(*turn((a + da) % 4, (b + db) % 4), core)
-
-    def block(da, db):
-        return block_of(*turn((a + da) % 4, (b + db) % 4))
-
-    own = block(0, 0)
-    mine = pl.ds(pl.multiple_of(core * rows, 16), rows)
-    theirs = pl.ds(pl.multiple_of(other * rows, 16), rows)
-    s_a = mail.slots((h, d) for h in range(2) for d in STEPS)
-    r_a = {d: mail.slot(2) for d in STEPS}
-    s_gate, s_own = mail.slot(), mail.slot()
     partner = device(y // 2 * 2 + 1 - grp, z, core)
     mail.start(s_gate, gps.at[1], gin, partner)
-    src = fc1.at[:, pl.ds(pl.multiple_of(other * half, 128), half)]
-    mail.start(s_own, src, gath.at[own, mine], sibling)
-    for d in STEPS:
-        for h in range(2):
-            to = device((y + d) % 4, z, 0) if h == 0 else device(y, (z + d) % 4, 1)
-            src = fc1.at[:, h * half : (h + 1) * half]
-            mail.start(s_a[h, d], src, gath.at[own, mine], to, r_a[d] + core)
-    gath[own, mine, :] = fc1[:, pl.ds(pl.multiple_of(core * half, 128), half)]
 
     loads[0].wait()
 

time: 115 us -> 115 us (level)
    pallas_call x1, Pallas kernels: 53.4 us -> 55.2 us  [forward(): pl.pallas_call(forward_kernel, out_shape=(shape((2 * rows, half), F32), s...]
where the time goes in v6:
time: 115 us; the launch traced here: 114 us
  Pallas kernels  114 us (99%)
    pallas_call x1, Pallas kernels, forward(): pl.pallas_call(forward_kernel, out_shape=(shape((2 * rows, half), F32), s...  55.2 us
    pallas_call x1, Pallas kernels, backward(): pl.pallas_call(backward_kernel, out_shape=(shape((here, 2 * half), F32),...  34.3 us
    pallas_call x1, Pallas kernels, middle(): pl.pallas_call(middle_kernel, out_shape=(shape((n_rows, here, width), F32...  22.1 us

profile of v6, /device:TPU:1, one launch (start us, length us, event | category | flops | bytes accessed | tf_op | source)
XLA Modules:
  0.0 114.4 jit_solution(15581418147423097624)
XLA Ops:
  0.6 55.2 %shard_map.130 = (f32[1024,640]{1,0:T(8,128)}, bf16[1024,640]{1,0:T(8,128)(2,1)}, f32[6,48,64]{2,1,0:T(8,128)}, bf16[640,64]{1,0:T(8,128)(2,1)}, f32[80,128]{1,0...) custom-call(bf16[512,2432]{1,0:T(8,128)(2,1)} %bitcast.12, ...), custom_call_target="tpu_custom_call" | custom-call | tf_op jit(solution)/shard_map/pallas_call | solution.py:507
  55.9 22.1 %shard_map.131 = (f32[4,32,64]{2,1,0:T(8,128)}, bf16[8,128,64]{2,1,0:T(8,128)(2,1)}) custom-call(f32[6,48,64]{2,1,0:T(8,128)} %get-tuple-element.23.sums, bf16[36,64,256]{2,1,0:T(8,128)(2,1)} %get-tuple-element.24.refs_0_, f32[20,2,160,128]{3,2,1,0:T(8,128)} %get-tuple-element.25.refs_1_, bf16[3,768,256]{2,1,0:T(8,128)(2,1)} %bitcast.11, ...), custom_call_target="tpu_custom_call" | custom-call | tf_op jit(solution)/shard_map/pallas_call | solution.py:716
  78.0 34.3 %shard_map.132 = (f32[76,1280]{1,0:T(8,128)}, f32[76,1280]{1,0:T(8,128)}) custom-call(bf16[16,160,1024]{2,1,0:T(8,128)(2,1)} %get-tuple-element.19.nrmt_hbm, f32[1024,640]{1,0:T(8,128)} %get-tuple-element.20.slope_hbm, bf16[1024,640]{1,0:T(8,128)(2,1)} %get-tuple-element.21.act_hbm, bf16[640,64]{1,0:T(8,128)(2,1)} %get-tuple-element.22.fold, ...), custom_call_target="tpu_custom_call" | custom-call | tf_op jit(solution)/shard_map/pallas_call | solution.py:873
  112.3 2.1 %shard_map.133 = (f32[76,1280]{1,0:T(8,128)}, f32[76,1280]{1,0:T(8,128)}, f32[4,32,64]{2,1,0:T(8,128)}) custom-call(f32[76,1280]{1,0:T(8,128)} %get-tuple-element.29.refs_0_, f32[76,1280]{1,0:T(8,128)} %get-tuple-element.30.refs_1_, f32[4,32,64]{2,1,0:T(8,128)} %get-tuple-element.31.refs_2_), custom_call_target="tpu_custom_call" | custom-call | tf_op jit(solution)/shard_map/pallas_call | solution.py:911
